TPU v7x, 128 devices: a whole 4x4x4 slice. The times are simulated.
128 devices in a mesh: section: 2 (over y_hi), dp: 8 (over z, y_lo), context: 8 (over x, core).
Axes of the slice: x: 4, y: 4 (y_hi: 2, y_lo: 2; y = y_hi * 2 + y_lo), z: 4, core: 2. Of those that a mesh axis runs over, the one named last changes fastest.
Arguments:
- tokens: bfloat16 [16, 1024, 576], P('dp', 'context'), may hold values from -6 to 6
- cotangent: bfloat16 [16, 1024, 576], P('dp', 'context'), may hold values from -6 to 6
- block_map: int32 [16, 16], P('dp'), may hold values from 0 to 15, each once within a row
- attention_gain: bfloat16 [2, 576], P('section', 'dp'), may hold values from 0.099609375 to 1.8984375
- query_weight: bfloat16 [2, 576, 576], P('section', 'dp'), may hold values from -0.25 to 0.25
- keyval_weight: bfloat16 [2, 576, 384], P('section', 'dp'), may hold values from -0.25 to 0.25
- output_weight: bfloat16 [2, 576, 576], P('section', 'dp'), may hold values from -0.75 to 0.75
- feedforward_gain: bfloat16 [2, 576], P('section', 'dp'), may hold values from 0.099609375 to 1.8984375
- gateup_weight: bfloat16 [2, 576, 3072], P('section', 'dp'), may hold values from -0.25 to 0.25
- down_weight: bfloat16 [2, 1536, 576], P('section', 'dp'), may hold values from -0.15625 to 0.15625
Outputs:
- hidden_states: bfloat16 [2, 16, 1024, 576], P('section', 'dp', 'context')
- input_grads: bfloat16 [2, 16, 1024, 576], P('section', 'dp', 'context')
- attention_gain_grads: float32 [2, 576], P('section', 'dp')
- query_grads: float32 [2, 576, 576], P('section', 'dp')
- keyval_grads: float32 [2, 576, 384], P('section', 'dp')
- output_grads: float32 [2, 576, 576], P('section', 'dp')
- feedforward_gain_grads: float32 [2, 576], P('section', 'dp')
- gateup_grads: float32 [2, 576, 3072], P('section', 'dp')
- down_grads: float32 [2, 1536, 576], P('section', 'dp')
Inputs may be any that keep to these rules, and one draw needn't show every extreme that they name: Each row is a permutation: stored block j of sequence s holds the sequence's block block_map[s, j].
All inputs are finite; a program needn't handle non-finite values.
Results may differ from a plain program's by a relative error of at most 0.028.
Values may be sent and summed in bfloat16 or wider, within the bound.
A program may use at most 192 MiB of HBM per device.

v0:
```python
import math

import jax
import jax.numpy as jnp
from jax import lax
from jax.sharding import Mesh
from jax.sharding import PartitionSpec as P

HEAD = 64
CONTEXT = ("context_0", "context_1")
DP = ("dp_0", "dp_1")


EPSILON = 1e-05
ROPE_BASE = 100000.0


def side_by_side(arrays, axis, dim, along):
    widths = [math.prod(a.shape[along:]) for a in arrays]
    both = jnp.concatenate(
        [a.reshape(*a.shape[:along], w) for a, w in zip(arrays, widths)], axis=along
    )
    out = lax.all_gather(both, axis, axis=dim, tiled=True)
    pieces = jnp.split(out, [sum(widths[:k]) for k in range(1, len(widths))], axis=along)
    return tuple((b.reshape(*out.shape[:along], *a.shape[along:]) for a, b in zip(arrays, pieces)))


def side_by_side_2(arrays, axis, dim, along):
    widths = [a.shape[along] for a in arrays]
    both = jnp.concatenate(arrays, axis=along)
    out = lax.all_gather(both, axis, axis=dim, tiled=True)
    return tuple(jnp.split(out, [sum(widths[:k]) for k in range(1, len(widths))], axis=along))


def in_one_piece(arrays, axis, dim, along):
    both = jnp.concatenate(arrays, axis=along)
    out, at, done = (lax.psum_scatter(both, axis, scatter_dimension=dim, tiled=True), 0, [])
    for a in arrays:
        done.append(lax.slice_in_dim(out, at, at + a.shape[along], axis=along))
        at += a.shape[along]
    return tuple(done)


def shifted(value, axis, steps):
    count = lax.axis_size(axis)
    first, last = (max(0, -steps), min(count, count - steps))
    return lax.ppermute(value, axis, [(source, source + steps) for source in range(first, last)])


def split_up(x, dim, devices):
    before, after = (x.shape[:dim], x.shape[dim + 1 :])
    return jnp.moveaxis(x.reshape(*before, devices, -1, *after), dim, 0)


def summed_rows(x, chips, core, dim):
    sizes = (lax.axis_size(chips), lax.axis_size(core))
    pieces = split_up(x, dim, sizes[0] * sizes[1])
    inside = pieces.shape[1:]
    pieces = pieces.reshape(*sizes, *inside).swapaxes(0, 1).reshape(-1, *inside)
    pieces = lax.psum_scatter(pieces, core, scatter_dimension=0, tiled=True)
    return lax.psum_scatter(pieces, chips, scatter_dimension=0, tiled=True)[0]


def from_everyone(x, axis):
    copies = jnp.broadcast_to(x, (lax.axis_size(axis), *x.shape))
    return lax.all_to_all(copies, axis, split_axis=0, concat_axis=0, tiled=True)


def in_order(pieces, dim):
    pieces = jnp.moveaxis(pieces, 0, dim)
    lengths = pieces.shape
    return pieces.reshape(*lengths[:dim], lengths[dim] * lengths[dim + 1], *lengths[dim + 2 :])


def gathered_copies(x, axis, dim):
    pieces = from_everyone(x, axis)
    return in_order(pieces, dim)


def rms_normed(values, gain):
    return values * lax.rsqrt(jnp.mean(values * values, axis=-1, keepdims=True) + EPSILON) * gain


def rope_tables(positions, head_size):
    half_size = head_size // 2
    freqs = ROPE_BASE ** (-2.0 * jnp.arange(half_size, dtype=jnp.float32) / head_size)
    angles = positions.astype(jnp.float32)[:, None] * freqs[None, :]
    return (jnp.cos(angles), jnp.sin(angles))


def rotate(values, cosine, sine):
    half_size = values.shape[-1] // 2
    first = values[..., :half_size]
    second = values[..., half_size:]
    cosine = cosine[:, None, :]
    sine = sine[:, None, :]
    return jnp.concatenate(
        [first * cosine - second * sine, second * cosine + first * sine], axis=-1
    )


def swiglu(gate_part, up_part):
    return jax.nn.silu(gate_part) * up_part


def body(
    tokens,
    cotangent,
    block_map,
    attention_gain,
    query_weight,
    keyval_weight,
    output_weight,
    feedforward_gain,
    gateup_weight,
    down_weight,
):
    section = lax.axis_index("section")
    context_index = lax.axis_index(CONTEXT)
    context_size = lax.axis_size(CONTEXT)
    dp_size = lax.axis_size(DP)
    gathered = (
        *side_by_side(
            (
                attention_gain,
                query_weight,
                keyval_weight,
                output_weight,
                feedforward_gain,
                gateup_weight,
            ),
            DP,
            1,
            2,
        ),
        lax.all_gather(down_weight, DP, axis=1, tiled=True),
    )
    gain_attn = gathered[0][0].astype(jnp.float32)
    w_query = gathered[1][0]
    w_keyval = gathered[2][0]
    w_output = gathered[3][0]
    gain_ffn = gathered[4][0].astype(jnp.float32)
    w_gateup = gathered[5][0]
    w_down = gathered[6][0]
    micro = tokens.shape[0]
    local = tokens.shape[1]
    width = tokens.shape[2]
    seq_len = local * context_size
    block_len = seq_len // block_map.shape[1]
    head_size = HEAD
    heads = width // head_size
    kv_width = w_keyval.shape[1] // 2
    kv_heads = kv_width // head_size
    group = heads // kv_heads
    hidden_width = w_down.shape[0]
    scale = head_size ** (-0.5)

    def positions(index):
        row = block_map[index]
        whole = (
            row[:, None] * block_len + jnp.arange(block_len, dtype=jnp.int32)[None, :]
        ).reshape(seq_len)
        own = lax.dynamic_slice_in_dim(whole, context_index * local, local)
        allowed = whole[None, :] <= own[:, None]
        cosine, sine = rope_tables(own, head_size)
        return (allowed, cosine, sine)

    def scores_of(rot_query, keys_all, allowed):
        grouped = rot_query.reshape(local, kv_heads, group, head_size)
        raw = (
            jnp.einsum(
                "lkgd,mkd->kglm",
                grouped,
                keys_all.reshape(seq_len, kv_heads, head_size),
                preferred_element_type=jnp.float32,
            )
            * scale
        )
        return jnp.where(allowed[None, None], raw, -jnp.inf)

    received = jnp.zeros((local, width), jnp.bfloat16)
    states = jnp.zeros((micro, local, width), jnp.bfloat16)
    kept_list = []
    for step_index in range(micro + 1):
        index = jnp.clip(step_index - section, 0, micro - 1)
        valid = (step_index - section >= 0) & (step_index - section < micro)
        source = jnp.where(section == 0, tokens[min(step_index, micro - 1)], received)
        forward_inputs = source.astype(jnp.float32)
        forward_allowed, forward_cosine, forward_sine = positions(index)
        forward_normed = rms_normed(forward_inputs, gain_attn).astype(jnp.bfloat16)
        queries = jnp.dot(forward_normed, w_query, preferred_element_type=jnp.float32)
        keyvals = jnp.dot(forward_normed, w_keyval, preferred_element_type=jnp.float32)
        forward_rot_query = rotate(
            queries.reshape(local, heads, head_size), forward_cosine, forward_sine
        ).astype(jnp.bfloat16)
        rot_keys = (
            rotate(
                keyvals[:, :kv_width].reshape(local, kv_heads, head_size),
                forward_cosine,
                forward_sine,
            )
            .astype(jnp.bfloat16)
            .reshape(local, kv_width)
        )
        values_low = keyvals[:, kv_width:].astype(jnp.bfloat16)
        forward_keys_all, forward_values_all = side_by_side_2((rot_keys, values_low), CONTEXT, 0, 1)
        forward_scores = scores_of(forward_rot_query, forward_keys_all, forward_allowed)
        top = jnp.max(forward_scores, axis=-1, keepdims=True)
        expo = jnp.exp(forward_scores - top)
        forward_total = jnp.sum(expo, axis=-1, keepdims=True)
        forward_logsum = top + jnp.log(forward_total)
        forward_probs = (expo / forward_total).astype(jnp.bfloat16)
        forward_attended = jnp.einsum(
            "kglm,mkd->lkgd",
            forward_probs,
            forward_values_all.reshape(seq_len, kv_heads, head_size),
            preferred_element_type=jnp.float32,
        )
        forward_attended = forward_attended.reshape(local, width).astype(jnp.bfloat16)
        forward_mixed = forward_inputs + jnp.dot(
            forward_attended, w_output, preferred_element_type=jnp.float32
        )
        forward_normed_ffn = rms_normed(forward_mixed, gain_ffn).astype(jnp.bfloat16)
        forward_gateup = jnp.dot(forward_normed_ffn, w_gateup, preferred_element_type=jnp.float32)
        forward_hidden = swiglu(
            forward_gateup[:, :hidden_width], forward_gateup[:, hidden_width:]
        ).astype(jnp.bfloat16)
        result = forward_mixed + jnp.dot(forward_hidden, w_down, preferred_element_type=jnp.float32)
        forward_saved = (
            forward_inputs,
            forward_normed,
            forward_rot_query,
            forward_keys_all,
            forward_values_all,
            forward_logsum,
            forward_attended,
            forward_mixed,
            forward_normed_ffn,
            forward_gateup,
            forward_hidden,
        )
        result, saved = (result, forward_saved)
        result_low = result.astype(jnp.bfloat16)
        states = jnp.where(valid, states.at[index].set(result_low), states)
        kept_list.append(saved)
        if step_index < micro:
            received = shifted(result_low, "section", 1)
    stacked = jax.tree.map(lambda *arrays: jnp.stack(arrays), *kept_list)
    totals = (
        jnp.zeros(gain_attn.shape, jnp.float32),
        jnp.zeros(w_query.shape, jnp.float32),
        jnp.zeros(w_keyval.shape, jnp.float32),
        jnp.zeros(w_output.shape, jnp.float32),
        jnp.zeros(gain_ffn.shape, jnp.float32),
        jnp.zeros(w_gateup.shape, jnp.float32),
        jnp.zeros(w_down.shape, jnp.float32),
    )
    back_received = jnp.zeros((local, width), jnp.bfloat16)
    in_grads = jnp.zeros((micro, local, width), jnp.bfloat16)
    for step_index in range(micro + 1):
        target = step_index - 1 + section
        valid = (target >= 0) & (target < micro)
        index = jnp.clip(target, 0, micro - 1)
        forward_step = jnp.clip(target + section, 0, micro)
        saved = jax.tree.map(lambda array: array[forward_step], stacked)
        incoming = jnp.where(section == 1, cotangent[min(step_index, micro - 1)], back_received)
        incoming = jnp.where(valid, incoming, jnp.zeros_like(incoming))
        (
            inputs,
            normed,
            backward_rot_query,
            backward_keys_all,
            values_all,
            logsum,
            attended,
            mixed,
            normed_ffn,
            gateup,
            hidden,
        ) = saved
        backward_allowed, backward_cosine, backward_sine = positions(index)
        down_grad = jnp.einsum("lf,ld->fd", hidden, incoming, preferred_element_type=jnp.float32)
        grad_hidden = jnp.einsum("ld,fd->lf", incoming, w_down, preferred_element_type=jnp.float32)
        _, pull = jax.vjp(swiglu, gateup[:, :hidden_width], gateup[:, hidden_width:])
        grad_gate, grad_up = pull(grad_hidden)
        grad_gateup = jnp.concatenate([grad_gate, grad_up], axis=1).astype(jnp.bfloat16)
        gateup_grad = jnp.einsum(
            "ld,lf->df", normed_ffn, grad_gateup, preferred_element_type=jnp.float32
        )
        grad_normed_ffn = jnp.einsum(
            "lf,df->ld", grad_gateup, w_gateup, preferred_element_type=jnp.float32
        )
        _, pull = jax.vjp(rms_normed, mixed, gain_ffn)
        grad_mixed, ffn_gain_grad = pull(grad_normed_ffn)
        grad_mixed = grad_mixed + incoming.astype(jnp.float32)
        grad_branch = grad_mixed.astype(jnp.bfloat16)
        output_grad = jnp.einsum(
            "ld,le->de", attended, grad_branch, preferred_element_type=jnp.float32
        )
        grad_attended = jnp.einsum(
            "le,de->ld", grad_branch, w_output, preferred_element_type=jnp.float32
        ).astype(jnp.bfloat16)
        scores = scores_of(backward_rot_query, backward_keys_all, backward_allowed)
        probs = jnp.exp(scores - logsum)
        grad_four = grad_attended.reshape(local, kv_heads, group, head_size)
        values_three = values_all.reshape(seq_len, kv_heads, head_size)
        keys_three = backward_keys_all.reshape(seq_len, kv_heads, head_size)
        grad_probs = jnp.einsum(
            "lkgd,mkd->kglm", grad_four, values_three, preferred_element_type=jnp.float32
        )
        inner = jnp.sum(probs * grad_probs, axis=-1, keepdims=True)
        grad_scores = (probs * (grad_probs - inner)).astype(jnp.bfloat16)
        grad_values = jnp.einsum(
            "kglm,lkgd->mkd",
            probs.astype(jnp.bfloat16),
            grad_four,
            preferred_element_type=jnp.float32,
        ).reshape(seq_len, kv_width)
        grad_keys = (
            jnp.einsum(
                "kglm,lkgd->mkd",
                grad_scores,
                backward_rot_query.reshape(local, kv_heads, group, head_size),
                preferred_element_type=jnp.float32,
            ).reshape(seq_len, kv_width)
            * scale
        )
        grad_query = (
            jnp.einsum(
                "kglm,mkd->lkgd", grad_scores, keys_three, preferred_element_type=jnp.float32
            ).reshape(local, heads, head_size)
            * scale
        )
        own_keys, own_values = tuple(
            (
                part.astype(jnp.float32)
                for part in in_one_piece(
                    (grad_keys.astype(jnp.bfloat16), grad_values.astype(jnp.bfloat16)),
                    CONTEXT,
                    0,
                    1,
                )
            )
        )
        grad_query = (
            rotate(grad_query, backward_cosine, -backward_sine)
            .reshape(local, width)
            .astype(jnp.bfloat16)
        )
        grad_keys_own = rotate(
            own_keys.reshape(local, kv_heads, head_size), backward_cosine, -backward_sine
        ).reshape(local, kv_width)
        grad_keyval = jnp.concatenate([grad_keys_own, own_values], axis=1).astype(jnp.bfloat16)
        query_grad = jnp.einsum("ld,le->de", normed, grad_query, preferred_element_type=jnp.float32)
        keyval_grad = jnp.einsum(
            "ld,le->de", normed, grad_keyval, preferred_element_type=jnp.float32
        )
        grad_normed = jnp.einsum(
            "le,de->ld", grad_query, w_query, preferred_element_type=jnp.float32
        )
        grad_normed = grad_normed + jnp.einsum(
            "le,de->ld", grad_keyval, w_keyval, preferred_element_type=jnp.float32
        )
        _, pull = jax.vjp(rms_normed, inputs, gain_attn)
        grad_inputs, attn_gain_grad = pull(grad_normed)
        grad_inputs = grad_inputs + grad_mixed
        grad_inputs, terms = (
            grad_inputs,
            (
                attn_gain_grad,
                query_grad,
                keyval_grad,
                output_grad,
                ffn_gain_grad,
                gateup_grad,
                down_grad,
            ),
        )
        totals = tuple((total + term for total, term in zip(totals, terms)))
        grad_low = grad_inputs.astype(jnp.bfloat16)
        in_grads = jnp.where(valid, in_grads.at[index].set(grad_low), in_grads)
        if step_index < micro:
            back_received = shifted(grad_low, "section", -1)
    pieces = [total.reshape(dp_size, -1) for total in totals]
    widths = [piece.shape[1] for piece in pieces]
    combined = jnp.concatenate(pieces, axis=1)
    finer = combined.reshape(dp_size * context_size, -1)
    share = summed_rows(finer, ("dp_0", "dp_1", "context_0"), "context_1", 0)
    share = gathered_copies(share.astype(jnp.bfloat16), CONTEXT, 1).astype(share.dtype)
    flat_share = share[0]
    outputs = []
    offset = 0
    for total, piece_width in zip(totals, widths):
        segment = flat_share[offset : offset + piece_width]
        offset = offset + piece_width
        shape = (1, total.shape[0] // dp_size) + tuple(total.shape[1:])
        outputs.append(segment.reshape(shape))
    return (
        states[None],
        in_grads[None],
        outputs[0],
        outputs[1],
        outputs[2],
        outputs[3],
        outputs[4],
        outputs[5],
        outputs[6],
    )


def solution(mesh):
    torus = Mesh(
        mesh.devices.reshape(mesh.shape["section"], 4, 2, 4, 2),
        ("section", "dp_0", "dp_1", "context_0", "context_1"),
    )
    return jax.shard_map(
        body,
        mesh=torus,
        in_specs=(
            P(DP, CONTEXT, None),
            P(DP, CONTEXT, None),
            P(DP, None),
            P("section", DP),
            P("section", DP, None),
            P("section", DP, None),
            P("section", DP, None),
            P("section", DP),
            P("section", DP, None),
            P("section", DP, None),
        ),
        out_specs=(
            P("section", DP, CONTEXT, None),
            P("section", DP, CONTEXT, None),
            P("section", DP),
            P("section", DP, None),
            P("section", DP, None),
            P("section", DP, None),
            P("section", DP),
            P("section", DP, None),
            P("section", DP, None),
        ),
        check_vma=False,
    )
```

profile of v0, /device:TPU:1, one launch (start us, length us, event | category | flops | bytes accessed | tf_op | source)
XLA Modules:
  0.0 888.0 jit_solution(17476920763970802206)
XLA Ops:
  8.8 2.4 concatenate.178
  24.6 104.0 %all-gather.3.cloned.1.call-done = bf16[1,576,4610]{2,1,0:T(8,128)(2,1)} async-done(((bf16[1,72,4610]{2,1,0:T(8,128)(2,1)}), bf16[1,576,4610]{2,1,0:T(8,128)(2,1)}) %all-gather.3.cloned.1.call-update) | async-done | bytes 5310736 | tf_op jit(solution)/shard_map/all_gather | solution.py:23
  132.8 14.6 %all_gather.16 = bf16[1024,384]{1,0:T(8,128)(2,1)S(1)} all-gather(bf16[128,384]{1,0:T(8,128)(2,1)S(1)} %pad_maximum_fusion.24), channel_id=1, replica_groups=mesh['section'=2,'dp_0'=4,'dp_1'=2,'context_0'=4,'context_1'=2] {'contex..., dimensions={0}, use_global_device_ids=true | all-gather | bytes 884736 | tf_op jit(solution)/shard_map/all_gather | solution.py:31
  159.2 21.2 %all-gather.5.cloned.1.call-done = bf16[1,1536,576]{2,1,0:T(8,128)(2,1)} async-done(((bf16[1,192,576]{2,1,0:T(8,128)(2,1)}), bf16[1,1536,576]{2,1,0:T(8,128)(2,1)}) %all-gather.5.cloned.1.call-update) | async-done | bytes 1769488 | tf_op jit(solution)/shard_map/all_gather | solution.py:136
  180.4 3.1 bitcast_dynamic-update-slice_fusion.1
  183.6 4.4 collective-permute-start
  194.0 15.8 %all_gather.18 = bf16[1024,384]{1,0:T(8,128)(2,1)S(1)} all-gather(bf16[128,384]{1,0:T(8,128)(2,1)S(1)} %pad_maximum_fusion.25), channel_id=1, replica_groups=mesh['section'=2,'dp_0'=4,'dp_1'=2,'context_0'=4,'context_1'=2] {'contex..., dimensions={0}, use_global_device_ids=true | all-gather | bytes 884736 | tf_op jit(solution)/shard_map/all_gather | solution.py:31
  225.2 5.6 collective-permute-start.1
  231.4 2.5 collective-permute-done.1
  236.9 14.6 %all_gather.19 = bf16[1024,384]{1,0:T(8,128)(2,1)S(1)} all-gather(bf16[128,384]{1,0:T(8,128)(2,1)S(1)} %pad_maximum_fusion.26), channel_id=1, replica_groups=mesh['section'=2,'dp_0'=4,'dp_1'=2,'context_0'=4,'context_1'=2] {'contex..., dimensions={0}, use_global_device_ids=true | all-gather | bytes 884736 | tf_op jit(solution)/shard_map/all_gather | solution.py:31
  263.0 2.1 dynamic-slice_bitcast_fusion
  266.2 2.9 fusion.183
  278.9 2.2 fusion.321
  294.6 2.1 copy.139
  298.0 2.1 copy.144
  306.2 2.7 fusion.130
  309.0 4.0 fusion.133
  313.0 2.4 fusion.140
  315.4 3.0 fusion.343
  318.4 3.0 fusion.344
  324.7 2.1 fusion.179
  328.3 2.6 bitcast_dynamic-update-slice_fusion
  332.9 5.4 collective-permute-done.2
  339.2 2.9 fusion.119
  342.9 2.2 fusion.175
  354.9 2.3 fusion.126
  357.2 2.4 fusion.210
  359.7 5.2 fusion.132
  364.9 3.5 fusion.138
  368.3 15.3 %reduce-scatter.16.cloned.1.call-done = bf16[128,384]{1,0:T(8,128)(2,1)} async-done(((bf16[1024,384]{1,0:T(8,128)(2,1)}), bf16[128,384]{1,0:T(8,128)(2,1)}) %reduce-scatter.16.cloned.1.call-update) | async-done | bytes 98320
  385.6 2.2 fusion.171
  388.5 2.8 fusion.190
  393.5 5.2 collective-permute-done.3
  399.7 2.9 fusion.122
  402.6 2.3 fusion.167
  411.4 2.3 copy.184
  413.9 3.5 add_add_fusion.2
  417.4 2.8 reshape.1512
  420.2 9.5 %add_add_fusion = f32[576,3072]{1,0:T(8,128)} fusion(f32[576,3072]{1,0:T(8,128)} %fusion.133, f32[576,3072]{1,0:T(8,128)} %fusion.132, bf16[128,1536]{1,0:T(8,128)(2,1)} %copy-done.90, bf16[128,1536]{1,0:T(8,128)(2,1)} %copy-done.89, bf16[3,128,576]{1,2,0:T(8,128)(2,1)} %copy-done.37, s32[]{:T(128)S(6)} %min.54), kind=kOutput, calls=%fused_computation | convolution fusion | flops 458096640 | bytes 22167556 | tf_op jit(solution)/shard_map/ld,lf->df/dot_general | solution.py:287
  429.9 7.2 reshape.1513
  437.1 5.7 add_add_fusion.1
  442.8 5.3 copy.148
  448.1 5.8 reshape.1514
  476.8 5.0 dynamic-update-slice.27
  481.8 3.7 dynamic-update-slice.28
  485.5 5.0 dynamic-update-slice.29
  491.9 20.5 %dynamic-update-slice.31 = f32[8,442512]{1,0:T(8,128)} dynamic-update-slice(f32[8,442512]{1,0:T(8,128)} %dynamic-update-slice.30, f32[8,221184]{1,0:T(8,128)} %reshape.1513, s32[]{} %constant.237, s32[]{} %constant.242) | dynamic-update-slice | bytes 14155780
  512.4 10.1 %dynamic-update-slice.32 = f32[8,442512]{1,0:T(8,128)} dynamic-update-slice(f32[8,442512]{1,0:T(8,128)} %dynamic-update-slice.31, f32[8,110592]{1,0:T(8,128)S(1)} %copy-done, s32[]{} %constant.237, s32[]{} %constant.243) | dynamic-update-slice | bytes 7077892 | tf_op jit(solution)/shard_map/concatenate | solution.py:386
  522.6 18.0 %reshape.1584 = f32[3540096]{0:T(1024)} reshape(f32[8,442512]{1,0:T(8,128)} %dynamic-update-slice.32) | data formatting | bytes 28320768
  540.6 26.0 %reshape.1585 = f32[1,32,2,55314]{3,2,1,0:T(2,128)} reshape(f32[3540096]{0:T(1024)} %reshape.1584) | data formatting | bytes 28320768
  566.6 10.4 %bitcast_bitcast_fusion = f32[2,32,1,55314]{3,0,1,2:T(2,128)} fusion(f32[1,32,2,55314]{3,2,1,0:T(2,128)} %reshape.1585), kind=kLoop, calls=%fused_computation.573 | loop fusion | bytes 28320768 | tf_op jit(solution)/shard_map/transpose | solution.py:59
  577.0 10.9 %copy.149 = f32[2,32,1,55314]{3,1,0,2:T(8,128)} copy(f32[2,32,1,55314]{3,0,1,2:T(2,128)} %bitcast_bitcast_fusion) | data formatting | bytes 28320768 | tf_op jit(solution)/shard_map/transpose | solution.py:59
  589.8 26.2 %reduce-scatter.12.cloned.1.call-done = f32[32,1,55314]{2,0,1:T(8,128)} async-done(((f32[64,1,55314]{2,0,1:T(8,128)}), f32[32,1,55314]{2,0,1:T(8,128)}) %reduce-scatter.12.cloned.1.call-update) | async-done | bytes 7080208 | tf_op jit(solution)/shard_map/reduce_scatter | solution.py:60
  616.0 182.2 %all-reduce.2 = bf16[32,1,55314]{2,0,1:T(8,128)(2,1)} all-reduce(f32[32,1,55314]{2,0,1:T(8,128)} %reduce-scatter.12.cloned.1.call-done), channel_id=6, replica_groups=mesh['section'=2,'dp_0'=4,'dp_1'=2,'context_0'=4,'context_1'=2] {'dp_0',..., use_global_device_ids=true, to_apply=%region_43.44.clone | all-reduce | flops 1770048 | bytes 10620288
  798.2 2.6 fusion.185
  802.2 7.0 reduce.72
  809.2 3.0 reshape.1586
  812.2 25.7 %all-to-all-start = ((bf16[8,2,27657]{2,1,0:T(2,128)(2,1)}), bf16[8,2,27657]{2,1,0:T(2,128)(2,1)}, u32[]{:S(2)}, u32[]{:S(2)}) async-start(bf16[8,2,27657]{2,1,0:T(2,128)(2,1)} %reshape.1586), calls=%async_computation.1 | async-start | bytes 1777664 | tf_op jit(solution)/shard_map/all_to_all | solution.py:66
  837.9 3.8 fusion.111
  845.3 6.1 all-to-all-done
  851.4 5.5 reshape.1587
  856.9 4.9 convert_reduce_fusion
  861.8 2.6 reshape.1530
  866.1 9.5 %slice_reduce_fusion = f32[221184]{0:T(1024)S(1)} fusion(f32[1,442512]{1,0:T(1,128)S(1)} %reshape.1530), kind=kLoop, calls=%fused_computation.128 | loop fusion | bytes 1769472 | tf_op jit(solution)/shard_map/slice | solution.py:394
  (543 shorter events, 166.6 us)
Async XLA Ops:
  7.2 121.4 %all-gather.3.cloned.1.call-start = ((), (), s32[]{:S(2)}) async-start(), calls=%async_computation.5 | async-start | bytes 6137856 | tf_op jit(solution)/shard_map/all_gather | solution.py:23
  11.2 169.2 %all-gather.5.cloned.1.call-start = ((), (), s32[]{:S(2)}) async-start(), calls=%async_computation.6 | async-start | bytes 2211840 | tf_op jit(solution)/shard_map/all_gather | solution.py:136
  12.0 310.1 %reduce-scatter.14.cloned.1.call-start = ((), (), s32[]{:S(2)}) async-start(), calls=%async_computation.8 | async-start | bytes 884736
  130.8 20.1 %copy-start.28 = (bf16[1,128,576]{1,2,0:T(8,128)(2,1)}, bf16[1,128,576]{1,2,0:T(8,128)(2,1)S(1)}, u32[]{:S(2)}) copy-start(bf16[1,128,576]{1,2,0:T(8,128)(2,1)S(1)} %multiply_convert_fusion.6) | copy-start | bytes 442372
  154.7 28.9 %copy-start.93 = (bf16[3,64,3,128]{3,1,2,0:T(8,128)(2,1)}, bf16[3,64,3,128]{3,1,2,0:T(8,128)(2,1)S(1)}, u32[]{:S(2)}) copy-start(bf16[3,64,3,128]{3,1,2,0:T(8,128)(2,1)S(1)} %fusion.98) | copy-start | bytes 442372
  156.4 27.1 %copy-start.15 = (f32[128,576]{0,1:T(8,128)}, f32[128,576]{0,1:T(8,128)S(1)}, u32[]{:S(2)}) copy-start(f32[128,576]{0,1:T(8,128)S(1)} %get-tuple-element.233) | copy-start | bytes 884740
  156.4 27.1 %copy-start.112 = (f32[128]{0:T(128)}, f32[128]{0:T(128)S(1)}, u32[]{:S(2)}) copy-start(f32[128]{0:T(128)S(1)} %add_rsqrt_fusion.4) | copy-start | bytes 1540
  180.4 13.4 %copy-start.101 = (f32[128,32]{0,1:T(8,128)S(1)}, f32[128,32]{0,1:T(8,128)}, u32[]{:S(2)}) copy-start(f32[128,32]{0,1:T(8,128)} %get-tuple-element.219) | copy-start | bytes 49156
  183.6 6.4 collective-permute-start
  220.7 39.8 %copy-start.18 = (f32[128,576]{0,1:T(8,128)}, f32[128,576]{0,1:T(8,128)S(1)}, u32[]{:S(2)}) copy-start(f32[128,576]{0,1:T(8,128)S(1)} %get-tuple-element.239) | copy-start | bytes 884740
  222.5 12.7 %copy-start.3 = (f32[128,3072]{1,0:T(8,128)}, f32[128,3072]{1,0:T(8,128)S(1)}, u32[]{:S(2)}) copy-start(f32[128,3072]{1,0:T(8,128)S(1)} %fusion.52) | copy-start | bytes 4718596
  222.5 11.4 %copy-start.35 = (bf16[2,128,576]{1,2,0:T(8,128)(2,1)S(1)}, bf16[2,128,576]{1,2,0:T(8,128)(2,1)}, u32[]{:S(2)}) copy-start(bf16[2,128,576]{1,2,0:T(8,128)(2,1)} %param.22) | copy-start | bytes 884740
  223.5 13.1 %copy-start.99 = (f32[128,32]{0,1:T(8,128)S(1)}, f32[128,32]{0,1:T(8,128)}, u32[]{:S(2)}) copy-start(f32[128,32]{0,1:T(8,128)} %get-tuple-element.220) | copy-start | bytes 49156
  223.5 13.1 %copy-start.100 = (f32[128,32]{0,1:T(8,128)S(1)}, f32[128,32]{0,1:T(8,128)}, u32[]{:S(2)}) copy-start(f32[128,32]{0,1:T(8,128)} %get-tuple-element.221) | copy-start | bytes 49156
  225.1 10.2 %copy-start.61 = (bf16[2,128,576]{1,2,0:T(8,128)(2,1)}, bf16[2,128,576]{1,2,0:T(8,128)(2,1)S(1)}, u32[]{:S(2)}) copy-start(bf16[2,128,576]{1,2,0:T(8,128)(2,1)S(1)} %get-tuple-element.240) | copy-start | bytes 884740
  225.2 8.7 collective-permute-start.1
  234.7 20.1 %copy-start.107 = (f32[128]{0:T(128)}, f32[128]{0:T(128)S(1)}, u32[]{:S(2)}) copy-start(f32[128]{0:T(128)S(1)} %add_rsqrt_fusion.1) | copy-start | bytes 1540
  262.4 28.4 %copy-start.1 = (f32[128,3072]{1,0:T(8,128)}, f32[128,3072]{1,0:T(8,128)S(1)}, u32[]{:S(2)}) copy-start(f32[128,3072]{1,0:T(8,128)S(1)} %fusion.51) | copy-start | bytes 4718596
  271.3 7.5 copy-start.14
  271.3 7.5 copy-start.17
  271.3 7.5 copy-start.19
  271.3 7.5 copy-start.113
  271.3 7.5 copy-start.115
  291.9 169.6 %copy-start.5 = (f32[3,128,576]{1,2,0:T(8,128)}, f32[3,128,576]{1,2,0:T(8,128)S(1)}, u32[]{:S(2)}) copy-start(f32[3,128,576]{1,2,0:T(8,128)S(1)} %pad_maximum_fusion.5) | copy-start | bytes 2654212
  291.9 9.5 %copy-start.23 = (f32[128,576]{0,1:T(8,128)S(1)}, f32[128,576]{0,1:T(8,128)}, u32[]{:S(2)}) copy-start(f32[128,576]{0,1:T(8,128)} %copy-done.22) | copy-start | bytes 884740
  292.6 10.3 %copy-start.98 = (f32[128,32]{0,1:T(8,128)S(1)}, f32[128,32]{0,1:T(8,128)}, u32[]{:S(2)}) copy-start(f32[128,32]{0,1:T(8,128)} %get-tuple-element.222) | copy-start | bytes 49156
  293.8 9.1 %copy-start.42 = (f32[3,64,3,128]{3,1,2,0:T(8,128)S(1)}, f32[3,64,3,128]{3,1,2,0:T(8,128)}, u32[]{:S(2)}) copy-start(f32[3,64,3,128]{3,1,2,0:T(8,128)} %convolution_multiply_fusion.2) | copy-start | bytes 884740
  293.8 11.0 %copy-start.43 = (bf16[1,128,1536]{2,1,0:T(8,128)(2,1)S(1)}, bf16[1,128,1536]{2,1,0:T(8,128)(2,1)}, u32[]{:S(2)}) copy-start(bf16[1,128,1536]{2,1,0:T(8,128)(2,1)} %fusion.397) | copy-start | bytes 1179652
  293.8 89.8 %reduce-scatter.16.cloned.1.call-start = ((), (), s32[]{:S(2)}) async-start(), calls=%async_computation.9 | async-start | bytes 884736
  294.6 20.8 %copy-start.11 = (bf16[1,1024,192]{1,2,0:T(8,128)(2,1)}, bf16[1,1024,192]{1,2,0:T(8,128)(2,1)S(1)}, u32[]{:S(2)}) copy-start(bf16[1,1024,192]{1,2,0:T(8,128)(2,1)S(1)} %copy.138) | copy-start | bytes 1179652
  298.0 20.4 %copy-start.10 = (bf16[1,1024,192]{1,2,0:T(8,128)(2,1)}, bf16[1,1024,192]{1,2,0:T(8,128)(2,1)S(1)}, u32[]{:S(2)}) copy-start(bf16[1,1024,192]{1,2,0:T(8,128)(2,1)S(1)} %copy.143) | copy-start | bytes 1179652
  298.0 11.0 %copy-start.84 = (bf16[128,1536]{1,0:T(8,128)(2,1)S(1)}, bf16[128,1536]{1,0:T(8,128)(2,1)}, u32[]{:S(2)}) copy-start(bf16[128,1536]{1,0:T(8,128)(2,1)} %copy-done.83) | copy-start | bytes 1179652
  300.2 8.8 copy-start.86
  304.8 8.2 copy-start.37
  318.4 24.5 %slice-start.10 = ((s8[5455872]{0:T(1024)(128)(4,1)}), s8[1261568]{0:T(1024)(128)(4,1)S(1)}, s32[]{:S(2)}) async-start(s8[5455872]{0:T(1024)(128)(4,1)} %bitcast.736), calls=%async_computation.21 | async-start | bytes 2523136
  326.8 12.4 %copy-start.119 = (f32[128]{0:T(128)}, f32[128]{0:T(128)S(1)}, u32[]{:S(2)}) copy-start(f32[128]{0:T(128)S(1)} %get-tuple-element.100) | copy-start | bytes 1540
  326.8 16.0 %copy-start.8 = (f32[3,128,576]{1,2,0:T(8,128)S(1)}, f32[3,128,576]{1,2,0:T(8,128)}, u32[]{:S(2)}) copy-start(f32[3,128,576]{1,2,0:T(8,128)} %copy-done.7) | copy-start | bytes 2654212
  326.8 16.0 %copy-start.121 = (f32[128]{0:T(128)S(1)}, f32[128]{0:T(128)}, u32[]{:S(2)}) copy-start(f32[128]{0:T(128)} %fusion.288) | copy-start | bytes 1540
  328.3 14.6 %slice-start.11 = ((s8[5455872]{0:T(1024)(128)(4,1)}), s8[4194304]{0:T(1024)(128)(4,1)S(1)}, s32[]{:S(2)}) async-start(s8[5455872]{0:T(1024)(128)(4,1)} %bitcast.736), calls=%async_computation.22 | async-start | bytes 8388608
  330.9 7.4 collective-permute-start.2
  353.2 104.8 %reduce-scatter.18.cloned.1.call-start = ((), (), s32[]{:S(2)}) async-start(), calls=%async_computation.10 | async-start | bytes 884736
  364.9 37.7 %slice-start.12 = ((s8[5455872]{0:T(1024)(128)(4,1)}), s8[1261568]{0:T(1024)(128)(4,1)S(1)}, s32[]{:S(2)}) async-start(s8[5455872]{0:T(1024)(128)(4,1)} %bitcast.738), calls=%async_computation.23 | async-start | bytes 2523136
  384.7 8.8 copy-start.75
  385.6 7.9 copy-start.76
  387.8 14.8 %copy-start.123 = (f32[128]{0:T(128)S(1)}, f32[128]{0:T(128)}, u32[]{:S(2)}) copy-start(f32[128]{0:T(128)} %fusion.290) | copy-start | bytes 1540
  388.5 14.1 %slice-start.13 = ((s8[5455872]{0:T(1024)(128)(4,1)}), s8[4194304]{0:T(1024)(128)(4,1)S(1)}, s32[]{:S(2)}) async-start(s8[5455872]{0:T(1024)(128)(4,1)} %bitcast.738), calls=%async_computation.24 | async-start | bytes 8388608
  391.3 7.4 collective-permute-start.3
  413.7 202.4 %reduce-scatter.12.cloned.1.call-start = ((), (), s32[]{:S(2)}) async-start(), calls=%async_computation.7 | async-start | bytes 21282816 | tf_op jit(solution)/shard_map/reduce_scatter | solution.py:60
  420.2 9.5 %copy-start.108 = (f32[576]{0:T(1024)S(1)}, f32[576]{0:T(1024)}, u32[]{:S(2)}) copy-start(f32[576]{0:T(1024)} %get-tuple-element.87) | copy-start | bytes 6916
  420.2 9.5 %copy-start.109 = (f32[576]{0:T(1024)S(1)}, f32[576]{0:T(1024)}, u32[]{:S(2)}) copy-start(f32[576]{0:T(1024)} %get-tuple-element.85) | copy-start | bytes 6916
  420.2 9.5 %copy-start.110 = (f32[576]{0:T(1024)S(1)}, f32[576]{0:T(1024)}, u32[]{:S(2)}) copy-start(f32[576]{0:T(1024)} %get-tuple-element.89) | copy-start | bytes 6916
  455.4 7.5 copy-start.29
  455.4 7.6 copy-start.71
  456.3 10.4 %copy-start.104 = (f32[576]{0:T(1024)S(1)}, f32[576]{0:T(1024)}, u32[]{:S(2)}) copy-start(f32[576]{0:T(1024)} %get-tuple-element.93) | copy-start | bytes 6916
  456.3 10.4 %copy-start.105 = (f32[576]{0:T(1024)S(1)}, f32[576]{0:T(1024)}, u32[]{:S(2)}) copy-start(f32[576]{0:T(1024)} %get-tuple-element.91) | copy-start | bytes 6916
  471.3 14.2 %copy-start.6 = (f32[8,41472]{1,0:T(8,128)S(1)}, f32[8,41472]{1,0:T(8,128)}, u32[]{:S(2)}) copy-start(f32[8,41472]{1,0:T(8,128)} %reshape.1512) | copy-start | bytes 3981316
  491.9 20.5 %copy-start = (f32[8,110592]{1,0:T(8,128)S(1)}, f32[8,110592]{1,0:T(8,128)}, u32[]{:S(2)}) copy-start(f32[8,110592]{1,0:T(8,128)} %reshape.1514) | copy-start | bytes 10616836
  798.2 39.7 %copy-start.2 = (f32[128,3072]{1,0:T(8,128)S(1)}, f32[128,3072]{1,0:T(8,128)}, u32[]{:S(2)}) copy-start(f32[128,3072]{1,0:T(8,128)} %copy-done.1) | copy-start | bytes 4718596
  809.2 33.5 %copy-start.118 = (f32[128]{0:T(128)S(1)}, f32[128]{0:T(128)}, u32[]{:S(2)}) copy-start(f32[128]{0:T(128)} %copy-done.117) | copy-start | bytes 1540
  809.2 33.5 %copy-start.120 = (f32[128]{0:T(128)S(1)}, f32[128]{0:T(128)}, u32[]{:S(2)}) copy-start(f32[128]{0:T(128)} %get-tuple-element.198) | copy-start | bytes 1540
  809.2 33.5 %copy-start.21 = (f32[128,576]{0,1:T(8,128)S(1)}, f32[128,576]{0,1:T(8,128)}, u32[]{:S(2)}) copy-start(f32[128,576]{0,1:T(8,128)} %copy-done.20) | copy-start | bytes 884740
  809.2 33.5 %copy-start.25 = (f32[128,576]{0,1:T(8,128)S(1)}, f32[128,576]{0,1:T(8,128)}, u32[]{:S(2)}) copy-start(f32[128,576]{0,1:T(8,128)} %copy-done.24) | copy-start | bytes 884740
  809.2 33.6 %copy-start.111 = (f32[128]{0:T(128)S(1)}, f32[128]{0:T(128)}, u32[]{:S(2)}) copy-start(f32[128]{0:T(128)} %fusion.291) | copy-start | bytes 1540
  812.2 39.2 %all-to-all-start = ((bf16[8,2,27657]{2,1,0:T(2,128)(2,1)}), bf16[8,2,27657]{2,1,0:T(2,128)(2,1)}, u32[]{:S(2)}, u32[]{:S(2)}) async-start(bf16[8,2,27657]{2,1,0:T(2,128)(2,1)} %reshape.1586), calls=%async_computation.1 | async-start | bytes 1777664 | tf_op jit(solution)/shard_map/all_to_all | solution.py:66
  (93 other events, 306.5 us)
Sparse Core Ops, SparseCore 0:
  11.3 117.1 all-gather.2
  130.2 50.1 all-gather.4
  293.9 28.1 reduce-scatter.13
  353.3 30.2 reduce-scatter.15
  413.8 30.3 reduce-scatter.17
  588.0 27.9 reduce-scatter.11
where the time goes:
time: 895 us; the launch traced here: 888 us
  blocking collectives  227 us (25%)
  local copies, waits for them, and re-layouts  215 us (24%)
  waiting for transfers between devices  189 us (21%)
  matrix products  127 us (14%)
  other arithmetic  72.9 us (8%)
  starting transfers between devices  39.3 us (4%)
  between operations  16.9 us (2%)
    unnamed x1, blocking collectives  182 us
    all_gather x1, waiting for transfers between devices, side_by_side(): out = lax.all_gather(both, axis, axis=dim, tiled=True)  104 us
    unnamed x314, local copies, waits for them, and re-layouts  102 us
    all_gather x3, blocking collectives, side_by_side_2(): out = lax.all_gather(both, axis, axis=dim, tiled=True)  45 us
    reduce_scatter x1, waiting for transfers between devices, summed_rows(): pieces = lax.psum_scatter(pieces, core, scatter_dimension=0, tiled=True)  26.2 us
    all_to_all x1, starting transfers between devices, from_everyone(): return lax.all_to_all(copies, axis, split_axis=0, concat_axis=0, tiled=True)  25.7 us
    transpose x2, local copies, waits for them, and re-layouts, summed_rows(): pieces = pieces.reshape(*sizes, *inside).swapaxes(0, 1).reshape(-1, *inside)  21.3 us
    all_gather x1, waiting for transfers between devices, body(): lax.all_gather(down_weight, DP, axis=1, tiled=True)  21.2 us
  transfers between devices with their start and end apart: 11, of which 10 were waited for; matrix products, arithmetic and copies ran while one was open for 14% of the time, Pallas kernels for 0%

commit v1 on v0

v1 whole, which is shorter than its diff:
```python
import jax
import jax.numpy as jnp
from jax import lax
from jax.experimental import pallas as pl
from jax.experimental.pallas import tpu as pltpu
from jax.sharding import Mesh
from jax.sharding import PartitionSpec as P

CONTEXT = ("x", "core")
DP = ("z", "ylo")
EPSILON = 1e-05
ROPE_BASE = 100000.0
BF = jnp.bfloat16
F32 = jnp.float32
R = 128
D = 576
FF = 1536
MESH = pl.DeviceIdType.MESH

NT = (((1,), (1,)), ((), ()))
TN = (((0,), (0,)), ((), ()))


def mm(a, b):
    return jnp.dot(a, b, preferred_element_type=F32)


def mm_nt(a, b):
    return lax.dot_general(a, b, NT, preferred_element_type=F32)


def mm_tn(a, b):
    return lax.dot_general(a, b, TN, preferred_element_type=F32)


SCRATCH = dict(
    Wg=((2, D, 2 * FF), BF),
    Wq=((2, D, 1024), BF),
    Wo=((2, D, D), BF),
    Wd=((2, FF, D), BF),
    Gg=((2, D, 2 * FF), BF),
    Gq=((2, D, 1024), BF),
    Go=((2, D, D), BF),
    Gd=((2, FF, D), BF),
    Rg=((D, 2 * FF), BF),
    Rq=((D, 1024), BF),
    Ro=((D, D), BF),
    Rd=((FF, D), BF),
    Sg=((4, 72, 768), BF),
    Sq=((4, 72, 1024), BF),
    So=((4, 72, D), BF),
    Sd=((4, 192, D), BF),
    Zg=((3, 144, 768), BF),
    Yg=((3, 72, 768), BF),
    Yq=((3, 72, 1024), BF),
    Yo=((3, 72, D), BF),
    Yd=((3, 192, D), BF),
    Xq=((4, 72, 1024), BF),
    Xo=((4, 72, D), BF),
    Xd=((4, 192, D), BF),
    PR=((2, 9, R, 1024), BF),
    GU=((2, R, 2 * FF), BF),
    KV=((2, 1024, 384), BF),
    HID=((2, R, FF), BF),
    NRM=((2, R, D), BF),
    NF=((2, R, D), BF),
    ATT=((2, R, D), BF),
    QS=((2, R, D), BF),
    MIX=((2, R, D), F32),
    HSB=((2, R, D), BF),
    IGB=((2, R, D), BF),
    GGU=((R, 2 * FF), BF),
    ACC=((R, D), F32),
    DKV=((8, 384, R), BF),
    DS=((4, 384, R), BF),
    DT=((4, 384, R), BF),
    DX=((2, 3, 384, R), BF),
    COS=((R, R), F32),
    SIN=((R, R), F32),
    BIAS=((R, 1024), F32),
)
N_SEMS = 224


def mega(tok, cot, bm, wq, wo, wg, wd, hs, ig, oq, oo, og, od, *scratch):
    s = dict(zip(SCRATCH, scratch))
    ss, rs = scratch[-2], scratch[-1]
    sec = lax.axis_index("section")
    z = lax.axis_index("z")
    ylo = lax.axis_index("ylo")
    x = lax.axis_index("x")
    core = lax.axis_index("core")
    y = sec * 2 + ylo
    d = z * 2 + ylo
    ctx = x * 2 + core
    is0, is1 = core == 0, core == 1

    keys = {}

    def sem(key):
        if key not in keys:
            keys[key] = len(keys)
            assert len(keys) <= N_SEMS
        return keys[key]

    def at(dy=0, dz=0, dx=0, dc=0):
        yy = lax.rem(y + dy, 4)
        return (
            lax.div(yy, 2),
            lax.rem(z + dz, 4),
            lax.rem(yy, 2),
            lax.rem(x + dx, 4),
            lax.rem(core + dc, 2),
        )

    def cp(key, src, dst, where):
        i = sem(key)
        return pltpu.make_async_remote_copy(
            src_ref=src,
            dst_ref=dst,
            send_sem=ss.at[i],
            recv_sem=rs.at[i],
            device_id=where,
            device_id_type=MESH,
        )

    def rows(n, i):
        return pl.ds(pl.multiple_of(n * i, 16), n)

    def cols(n, i):
        return pl.ds(pl.multiple_of(n * i, 128), n)

    barrier = pltpu.get_barrier_semaphore()
    peers = [at(dy=k) for k in (1, 2, 3)] + [at(dz=k) for k in (1, 2, 3)]
    peers += [at(dx=k) for k in (1, 2, 3)] + [at(dc=1)]
    for p in peers:
        pl.semaphore_signal(barrier, inc=1, device_id=p, device_id_type=MESH)
    pl.semaphore_wait(barrier, len(peers))

    W = dict(q=s["Wq"], o=s["Wo"], d=s["Wd"])
    S = dict(q=s["Sq"], o=s["So"], d=s["Sd"])
    own = dict(q=wq, o=wo, d=wd)
    OTHERS = ("q", "o", "d")

    def ag_y(m, k):
        if m == "g":
            return cp(("ay", m, k), wg.at[:, cols(768, x)], s["Sg"].at[y], at(dy=k))
        if m == "d":
            return cp(("ay", m, k), wd, s["Wd"].at[sec, rows(192, d)], at(dy=k))
        return cp(("ay", m, k), own[m], S[m].at[y], at(dy=k))

    def ag_z(m, L, k):
        if m == "g":
            part = s["Wg"].at[L, rows(144, z), cols(768, x)]
        elif m == "d":
            part = s["Wd"].at[L, rows(384, z)]
        else:
            part = W[m].at[L, rows(144, z)]
        return cp(("az", m, L, k), part, part, at(dz=k))

    def ag_x(L, k):
        part = s["Wg"].at[L, :, cols(768, x)]
        return cp(("ax", L, k), part, part, at(dx=k))

    def ag_sib_g(L, k):
        part = s["Wg"].at[L, :, cols(768, lax.rem(x + 4 - k, 4))]
        return cp(("asg", L, k), part, part, at(dc=1))

    def ag_sib(m, L):
        part = W[m].at[L]
        return cp(("as", m, L), part, part, at(dc=1))

    def join(m, L):
        buf = s["Sg"] if m == "g" else S[m]
        both = jnp.concatenate([buf[2 * L].astype(F32), buf[2 * L + 1].astype(F32)], axis=0).astype(BF)
        if m == "g":
            s["Wg"][L, rows(144, z), cols(768, x)] = both
        else:
            W[m][L, rows(144, z), :] = both

    @pl.when(is1)
    def _():
        for m in OTHERS:
            for k in (1, 2, 3):
                ag_y(m, k).start()
        s["Sq"][y] = wq[...]
        s["So"][y] = wo[...]
        s["Wd"][sec, rows(192, d), :] = wd[...]

    @pl.when(is0)
    def _():
        for k in (1, 2, 3):
            ag_y("g", k).start()
        s["Sg"][y] = wg[:, cols(768, x)]

    lane = lax.broadcasted_iota(jnp.int32, (R, R), 1)
    row = lax.broadcasted_iota(jnp.int32, (R, R), 0)
    first = row < 64
    pos_t = jnp.where(first, bm[sec, 2 * ctx], bm[sec, 2 * ctx + 1]) * 64 + jnp.where(first, row, row - 64)
    freq = jnp.exp((lane % 32).astype(F32) * F32(-2.0 / 64 * jnp.log(ROPE_BASE)))
    angle = pos_t.astype(F32) * freq
    s["COS"][...] = jnp.cos(angle)
    sine = jnp.sin(angle)
    s["SIN"][...] = jnp.where(lane % 64 < 32, -sine, sine)
    pos_f = pos_t[:, :1].astype(F32)
    for j in range(16):
        u = lax.broadcasted_iota(jnp.int32, (R, 64), 1) + bm[sec, j] * 64
        s["BIAS"][:, 64 * j : 64 * j + 64] = jnp.where(u.astype(F32) <= pos_f, 0.0, -1e30).astype(F32)

    def ag_start_z(L):
        @pl.when(is1)
        def _():
            for m in OTHERS:
                if L == 0:
                    for k in (1, 2, 3):
                        ag_y(m, k).wait_recv()
                if m != "d":
                    join(m, L)
                for k in (1, 2, 3):
                    ag_z(m, L, k).start()

        @pl.when(is0)
        def _():
            if L == 0:
                for k in (1, 2, 3):
                    ag_y("g", k).wait_recv()
            join("g", L)
            for k in (1, 2, 3):
                ag_z("g", L, k).start()

    def ag_fwd_x(L):
        @pl.when(is0)
        def _():
            for k in (1, 2, 3):
                ag_z("g", L, k).wait_recv()
            for k in (1, 2, 3):
                ag_x(L, k).start()
            ag_sib_g(L, 0).start()

    def ag_fwd_sib(m, L):
        @pl.when(is1)
        def _():
            for k in (1, 2, 3):
                ag_z(m, L, k).wait_recv()
            ag_sib(m, L).start()

    def ag_fwd_sib_g(L):
        @pl.when(is0)
        def _():
            for k in (1, 2, 3):
                ag_x(L, k).wait_recv()
                ag_sib_g(L, k).start()

    def need(m, L):
        if m == "g":
            @pl.when(is1)
            def _():
                for k in (0, 1, 2, 3):
                    ag_sib_g(L, k).wait_recv()
        else:
            @pl.when(is0)
            def _():
                ag_sib(m, L).wait_recv()

    def ag_done():
        @pl.when(is1)
        def _():
            for m in OTHERS:
                for k in (1, 2, 3):
                    ag_y(m, k).wait_send()
                for L in (0, 1):
                    for k in (1, 2, 3):
                        ag_z(m, L, k).wait_send()
                    ag_sib(m, L).wait_send()

        @pl.when(is0)
        def _():
            for k in (1, 2, 3):
                ag_y("g", k).wait_send()
            for L in (0, 1):
                for k in (1, 2, 3):
                    ag_z("g", L, k).wait_send()
                    ag_x(L, k).wait_send()
                for k in (0, 1, 2, 3):
                    ag_sib_g(L, k).wait_send()

    def tiled(t, n):
        return jnp.concatenate([t] * n, axis=1)

    def swap(v):
        width = v.shape[1]
        ahead = pltpu.roll(v, width - 32, 1)
        behind = pltpu.roll(v, 32, 1)
        low = lax.broadcasted_iota(jnp.int32, v.shape, 1) % 64 < 32
        return jnp.where(low, ahead, behind)

    def gains(L):
        eye = (
            lax.broadcasted_iota(jnp.int32, (D, D), 0) == lax.broadcasted_iota(jnp.int32, (D, D), 1)
        ).astype(F32).astype(BF)
        both = mm_tn(s["Wq"][L, :, 896:1024], eye)
        return both[64:65], both[65:66]

    def kv_x(L, k):
        part = s["KV"].at[L, rows(R, ctx)]
        return cp(("kx", L, k), part, part, at(dx=k))

    def kv_sib(L, k):
        part = s["KV"].at[L, rows(R, lax.rem(x + 4 - k, 4) * 2 + core)]
        return cp(("ks", L, k), part, part, at(dc=1))

    def hs_send(L):
        return cp("hs", s["HSB"].at[L], hs.at[sec], at(dy=2))

    def ig_send(L):
        return cp("ig", s["IGB"].at[L], ig.at[sec], at(dy=2))

    def forward(L, xin, mid):
        need("q", L)
        gain_a, gain_f = gains(L)
        r = lax.rsqrt(jnp.mean(xin * xin, axis=1, keepdims=True) + EPSILON)
        normed = (xin * r * gain_a).astype(BF)
        s["NRM"][L] = normed
        qkv = mm(normed, s["Wq"][L])
        kq = qkv[:, :768]
        kq = kq * tiled(s["COS"][...], 6) + swap(kq) * tiled(s["SIN"][...], 6)
        s["KV"][L, rows(R, ctx), :] = jnp.concatenate([kq[:, :192], qkv[:, 768:960]], axis=1).astype(BF)
        for k in (1, 2, 3):
            kv_x(L, k).start()
        kv_sib(L, 0).start()
        s["QS"][L] = (kq[:, 192:768] * 0.125).astype(BF)
        mid[0]()
        for k in (1, 2, 3):
            kv_x(L, k).wait_recv()
            kv_sib(L, k).start()
        mid[1]()
        for k in (0, 1, 2, 3):
            kv_sib(L, k).wait_recv()
        outs = []
        for kh in range(3):
            keys_h = s["KV"][L, :, 64 * kh : 64 * kh + 64]
            vals_h = s["KV"][L, :, 192 + 64 * kh : 256 + 64 * kh]
            for h in range(3 * kh, 3 * kh + 3):
                sc = mm_nt(s["QS"][L, :, 64 * h : 64 * h + 64], keys_h) + s["BIAS"][...]
                e = jnp.exp(sc - jnp.max(sc, axis=1, keepdims=True))
                p = (e * (1.0 / jnp.sum(e, axis=1, keepdims=True))).astype(BF)
                s["PR"][L, h] = p
                outs.append(mm(p, vals_h))
        att = jnp.concatenate(outs, axis=1).astype(BF)
        s["ATT"][L] = att
        mid[2]()
        need("o", L)
        mixed = xin + mm(att, s["Wo"][L])
        s["MIX"][L] = mixed
        r = lax.rsqrt(jnp.mean(mixed * mixed, axis=1, keepdims=True) + EPSILON)
        s["NF"][L] = (mixed * r * gain_f).astype(BF)
        mid[3]()
        need("g", L)

        @pl.loop(0, 4)
        def _(q):
            nf = s["NF"][L]
            g = mm(nf, s["Wg"][L, :, cols(384, q)])
            u = mm(nf, s["Wg"][L, :, cols(384, q + 4)])
            s["GU"][L, :, cols(384, q)] = g.astype(BF)
            s["GU"][L, :, cols(384, q + 4)] = u.astype(BF)
            s["HID"][L, :, cols(384, q)] = (g / (1.0 + jnp.exp(-g)) * u).astype(BF)

        mid[4]()
        need("d", L)
        out = (s["MIX"][L] + mm(s["HID"][L], s["Wd"][L])).astype(BF)
        s["HSB"][L] = out

        @pl.when(sec == L)
        def _():
            hs[sec] = out

        @pl.when(sec != L)
        def _():
            hs_send(L).start()

    G = dict(q=s["Gq"], o=s["Go"], d=s["Gd"], g=s["Gg"])
    RAW = dict(q=s["Rq"], o=s["Ro"], d=s["Rd"], g=s["Rg"])
    WALL = dict(W, g=s["Wg"])
    ZN = dict(q=144, o=144, d=384)
    YR = dict(q=s["Yq"], o=s["Yo"], d=s["Yd"])
    XR = dict(q=s["Xq"], o=s["Xo"], d=s["Xd"])
    OUT = dict(q=oq, o=oo, d=od)

    def ra(m, L):
        return RAW[m] if L == 1 else WALL[m].at[1]

    def rz(m, L):
        return G[m].at[0] if L == 1 else RAW[m]

    def g_sib(m, L):
        return cp(("gs", m, L), G[m].at[L], ra(m, L), at(dc=1))

    def grad_out(m, L):
        @pl.when(is1 if m == "g" else is0)
        def _():
            g_sib(m, L).start()

    def add_sib(m, L):
        g_sib(m, L).wait_recv()
        ref, other = G[m].at[L], ra(m, L)
        n = ref.shape[0] // 4

        @pl.loop(0, 4)
        def _(i):
            t = rows(n, i)
            ref[t, :] = (ref[t, :].astype(F32) + other[t, :].astype(F32)).astype(BF)

    def gx(L, k):
        src = s["Gg"].at[L, :, cols(768, lax.rem(x + k, 4))]
        dst = (s["Gg"].at[0] if L == 1 else s["Rg"]).at[:, pl.ds(768 * (k - 1), 768)]
        return cp(("gx", L, k), src, dst, at(dx=k))

    def gz(L, k):
        src = s["Gg"].at[L, rows(144, lax.rem(z + k, 4)), cols(768, x)]
        dst = s["Zg"].at[k - 1] if L == 1 else s["Rg"].at[pl.ds(144 * (k - 1), 144), pl.ds(2304, 768)]
        return cp(("gz", L, k), src, dst, at(dz=k))

    def y_target(L, k):
        yy = lax.rem(y + k, 4)
        return lax.div(yy, 2) == L, lax.rem(yy, 2)

    def gy(L, k):
        _, half = y_target(L, k)
        return cp(("gy", L, k), s["Sg"].at[2 * L + half], s["Yg"].at[k - 1], at(dy=k))

    def gfx(L, k):
        part = og.at[:, cols(768, x)]
        return cp(("gfx", L, k), part, part, at(dx=k))

    def gfs(L, k):
        part = og.at[:, cols(768, lax.rem(x + 4 - k, 4))]
        return cp(("gfs", L, k), part, part, at(dc=1))

    def a1(L):
        @pl.when(is0)
        def _():
            add_sib("g", L)
            for k in (1, 2, 3):
                gx(L, k).start()

    def a2(L):
        @pl.when(is0)
        def _():
            for k in (1, 2, 3):
                gx(L, k).wait_recv()
            other = s["Gg"].at[0] if L == 1 else s["Rg"]

            @pl.loop(0, 4)
            def _(i):
                t = rows(144, i)
                total = s["Gg"][L, t, cols(768, x)].astype(F32)
                for k in range(3):
                    total = total + other[t, 768 * k : 768 * k + 768].astype(F32)
                s["Gg"][L, t, cols(768, x)] = total.astype(BF)

            for k in (1, 2, 3):
                gz(L, k).start()

    def a3(L):
        @pl.when(is0)
        def _():
            for k in (1, 2, 3):
                gz(L, k).wait_recv()
            total = s["Gg"][L, rows(144, z), cols(768, x)].astype(F32)
            for k in range(3):
                other = s["Zg"][k] if L == 1 else s["Rg"][144 * k : 144 * k + 144, 2304:]
                total = total + other.astype(F32)
            s["Sg"][2 * L] = total[:72].astype(BF)
            s["Sg"][2 * L + 1] = total[72:].astype(BF)
            for k in (1, 2, 3):
                @pl.when(y_target(L, k)[0])
                def _():
                    gy(L, k).start()

    def a4(L):
        @pl.when(is0 & (sec == L))
        def _():
            for k in (1, 2, 3):
                gy(L, k).wait_recv()
            total = s["Sg"][2 * L + ylo].astype(F32)
            for k in range(3):
                total = total + s["Yg"][k].astype(F32)
            og[:, cols(768, x)] = total
            for k in (1, 2, 3):
                gfx(L, k).start()
            gfs(L, 0).start()

    def a5(L):
        @pl.when(is0 & (sec == L))
        def _():
            for k in (1, 2, 3):
                gfx(L, k).wait_recv()
                gfs(L, k).start()

    def bz(m, L, k):
        n = ZN[m]
        src = G[m].at[L, rows(n, lax.rem(z + k, 4))]
        dst = rz(m, L).at[pl.ds(n * (k - 1), n)]
        return cp(("bz", m, L, k), src, dst, at(dz=k))

    def by(m, L, k):
        _, half = y_target(L, k)
        return cp(("by", m, L, k), S[m].at[2 * L + half], YR[m].at[k - 1], at(dy=k))

    def bx(m, L, k):
        return cp(("bx", m, L, k), XR[m].at[x], XR[m].at[x], at(dx=k))

    def bf(m, L):
        return cp(("bf", m, L), OUT[m], OUT[m], at(dc=1))

    def b1(m, L):
        @pl.when(is1)
        def _():
            add_sib(m, L)
            for k in (1, 2, 3):
                bz(m, L, k).start()

    def b2(m, L):
        n = ZN[m]

        @pl.when(is1)
        def _():
            for k in (1, 2, 3):
                bz(m, L, k).wait_recv()
            total = G[m][L, rows(n, z), :].astype(F32)
            for k in range(3):
                total = total + rz(m, L)[n * k : n * k + n, :].astype(F32)
            S[m][2 * L] = total[: n // 2].astype(BF)
            S[m][2 * L + 1] = total[n // 2 :].astype(BF)
            for k in (1, 2, 3):
                @pl.when(y_target(L, k)[0])
                def _():
                    by(m, L, k).start()

    def b3(m, L):
        @pl.when(is1 & (sec == L))
        def _():
            for k in (1, 2, 3):
                by(m, L, k).wait_recv()
            total = S[m][2 * L + ylo].astype(F32)
            for k in range(3):
                total = total + YR[m][k].astype(F32)
            XR[m][x] = total.astype(BF)
            for k in (1, 2, 3):
                bx(m, L, k).start()

    def b4(m, L):
        @pl.when(is1 & (sec == L))
        def _():
            for k in (1, 2, 3):
                bx(m, L, k).wait_recv()
            total = XR[m][0].astype(F32)
            for k in range(1, 4):
                total = total + XR[m][k].astype(F32)
            OUT[m][...] = total
            bf(m, L).start()

    def grads_done():
        for L in (0, 1):
            @pl.when(is0)
            def _():
                for m in OTHERS:
                    g_sib(m, L).wait_send()
                for k in (1, 2, 3):
                    gx(L, k).wait_send()
                    gz(L, k).wait_send()

                    @pl.when(y_target(L, k)[0])
                    def _():
                        gy(L, k).wait_send()

            @pl.when(is1)
            def _():
                g_sib("g", L).wait_send()
                for m in OTHERS:
                    for k in (1, 2, 3):
                        bz(m, L, k).wait_send()

                        @pl.when(y_target(L, k)[0])
                        def _():
                            by(m, L, k).wait_send()

            @pl.when(is0 & (sec == L))
            def _():
                for k in (1, 2, 3):
                    gfx(L, k).wait_send()
                for k in range(4):
                    gfs(L, k).wait_send()
                for m in OTHERS:
                    bf(m, L).wait_recv()

            @pl.when(is1 & (sec == L))
            def _():
                for m in OTHERS:
                    for k in (1, 2, 3):
                        bx(m, L, k).wait_send()
                    bf(m, L).wait_send()
                for k in range(4):
                    gfs(L, k).wait_recv()

    def dkv_sib(L, j):
        return cp(("ds", L, j), s["DKV"].at[2 * j + 1 - core], s["DS"].at[j], at(dc=1))

    def dkv_x(L, k):
        return cp(("dx", L, k), s["DT"].at[lax.rem(x + k, 4)], s["DX"].at[L, k - 1], at(dx=k))

    def backward(L, xin, dF, mid):
        gain_a, gain_f = gains(L)
        dlow = dF.astype(BF)
        if L == 1:
            s["IGB"][1] = dlow

        @pl.loop(0, 4)
        def _(q):
            up = s["IGB"][1]
            gh = mm_nt(up, s["Wd"][L, rows(384, q), :])
            g = s["GU"][L, :, cols(384, q)].astype(F32)
            u = s["GU"][L, :, cols(384, q + 4)].astype(F32)
            sig = 1.0 / (1.0 + jnp.exp(-g))
            s["GGU"][:, cols(384, q)] = (gh * u * (sig * (1.0 + g * (1.0 - sig)))).astype(BF)
            s["GGU"][:, cols(384, q + 4)] = (gh * (g * sig)).astype(BF)
            s["Gd"][L, rows(384, q), :] = mm_tn(s["HID"][L, :, cols(384, q)], up).astype(BF)

        grad_out("d", L)
        s["ACC"][...] = jnp.zeros((R, D), F32)

        @pl.loop(0, 4)
        def _(q):
            gg = s["GGU"][:, cols(768, q)]
            s["Gg"][L, :, cols(768, q)] = mm_tn(s["NF"][L], gg).astype(BF)
            s["ACC"][...] += mm_nt(gg, s["Wg"][L, :, cols(768, q)])

        grad_out("g", L)
        gnf = s["ACC"][...]
        mixed = s["MIX"][L]
        r = lax.rsqrt(jnp.mean(mixed * mixed, axis=1, keepdims=True) + EPSILON)
        e = gnf * gain_f
        z_ffn = (gnf * mixed * r).astype(BF)
        gm = dF + r * e - mixed * (r * r * r * jnp.mean(e * mixed, axis=1, keepdims=True))
        gb = gm.astype(BF)
        att = s["ATT"][L]
        s["Go"][L] = mm_tn(att, gb).astype(BF)
        grad_out("o", L)
        ga = mm_nt(gb, s["Wo"][L]).astype(BF)
        mid[0]()
        prod = ga.astype(F32) * att.astype(F32)
        gqs = []
        for kh in range(3):
            keys_h = s["KV"][L, :, 64 * kh : 64 * kh + 64]
            vals_h = s["KV"][L, :, 192 + 64 * kh : 256 + 64 * kh]
            dk = jnp.zeros((64, 1024), F32)
            dv = jnp.zeros((64, 1024), F32)
            for h in range(3 * kh, 3 * kh + 3):
                lanes = slice(64 * h, 64 * h + 64)
                ga_h = ga[:, lanes]
                p = s["PR"][L, h]
                inner = jnp.sum(prod[:, lanes], axis=1, keepdims=True)
                ds = (p.astype(F32) * (mm_nt(ga_h, vals_h) - inner)).astype(BF)
                dv = dv + mm_tn(ga_h, p)
                dk = dk + mm_tn(s["QS"][L, :, lanes], ds)
                gqs.append(mm(ds, keys_h) * 0.125)
            dk, dv = dk.astype(BF), dv.astype(BF)
            for c in range(8):
                s["DKV"][c, 64 * kh : 64 * kh + 64, :] = dk[:, R * c : R * c + R]
                s["DKV"][c, 192 + 64 * kh : 256 + 64 * kh, :] = dv[:, R * c : R * c + R]
        for j in range(4):
            dkv_sib(L, j).start()
        mid[1]()
        for j in range(4):
            dkv_sib(L, j).wait_recv()
            s["DT"][j] = (s["DKV"][2 * j + core].astype(F32) + s["DS"][j].astype(F32)).astype(BF)
        for k in (1, 2, 3):
            dkv_x(L, k).start()
        mid[2]()
        total = s["DT"][x].astype(F32)
        for k in (1, 2, 3):
            dkv_x(L, k).wait_recv()
            total = total + s["DX"][L, k - 1].astype(F32)
        for j in range(4):
            dkv_sib(L, j).wait_send()
        for k in (1, 2, 3):
            dkv_x(L, k).wait_send()
        gkv = total.T
        kq = jnp.concatenate([gkv[:, :192]] + gqs, axis=1)
        kq = kq * tiled(s["COS"][...], 6) - swap(kq) * tiled(s["SIN"][...], 6)
        gall = jnp.concatenate([kq, gkv[:, 192:], jnp.zeros((R, 64), F32)], axis=1).astype(BF)
        r = lax.rsqrt(jnp.mean(xin * xin, axis=1, keepdims=True) + EPSILON)
        gn = mm_nt(gall, s["Wq"][L])
        z_att = (gn * xin * r).astype(BF)
        sel = lax.broadcasted_iota(jnp.int32, (2 * R, 128), 1) - lax.broadcasted_iota(jnp.int32, (2 * R, 128), 0) // R
        tail = mm_tn(jnp.concatenate([z_att, z_ffn], axis=0), (sel == 64).astype(F32).astype(BF))
        gw = mm_tn(s["NRM"][L], gall)
        s["Gq"][L, :, :896] = gw[:, :896].astype(BF)
        s["Gq"][L, :, 896:] = (gw[:, 896:] + tail).astype(BF)
        grad_out("q", L)
        e = gn * gain_a
        dx = gm + r * e - xin * (r * r * r * jnp.mean(e * xin, axis=1, keepdims=True))
        low = dx.astype(BF)
        return low

    def put_ig(L, low):
        s["IGB"][1 if L == 1 else 0] = low

        @pl.when(sec == L)
        def _():
            ig[sec] = low

        @pl.when(sec != L)
        def _():
            ig_send(1 if L == 1 else 0).start()

    ag_start_z(0)
    ag_fwd_x(0)
    ag_fwd_sib("q", 0)

    def f00():
        ag_fwd_sib("o", 0)

    def f01():
        pass

    def f02():
        ag_fwd_sib("d", 0)
        ag_start_z(1)

    def f03():
        ag_fwd_sib_g(0)

    def f04():
        ag_fwd_sib("q", 1)
        ag_fwd_x(1)

    forward(0, tok[sec].astype(F32), (f00, f01, f02, f03, f04))

    def f10():
        ag_fwd_sib("o", 1)
        ag_fwd_sib("d", 1)

    def f13():
        ag_fwd_sib_g(1)

    none = lambda: None
    forward(1, s["HSB"][0].astype(F32), (f10, none, none, f13, none))
    ag_done()
    for L in (0, 1):
        for k in (1, 2, 3):
            kv_x(L, k).wait_send()
        for k in range(4):
            kv_sib(L, k).wait_send()

    def c10():
        a1(1)
        b1("d", 1)

    def c11():
        b1("o", 1)

    def c12():
        b2("d", 1)

    low = backward(1, s["HSB"][0].astype(F32), cot[sec].astype(F32), (c10, c11, c12))
    put_ig(1, low)
    b2("o", 1)
    a2(1)
    b1("q", 1)

    def c00():
        a3(1)
        b3("d", 1)
        b3("o", 1)
        a1(0)
        b1("d", 0)

    def c01():
        b2("q", 1)
        b1("o", 0)
        a4(1)
        b4("d", 1)
        b4("o", 1)

    def c02():
        b3("q", 1)
        a5(1)
        b2("d", 0)

    low = backward(0, tok[sec].astype(F32), s["IGB"][1].astype(F32), (c00, c01, c02))
    put_ig(0, low)
    b4("q", 1)
    b1("q", 0)
    b2("o", 0)
    a2(0)
    b2("q", 0)
    b3("d", 0)
    b3("o", 0)
    a3(0)
    b3("q", 0)
    b4("d", 0)
    b4("o", 0)
    a4(0)
    b4("q", 0)
    a5(0)
    grads_done()

    @pl.when(sec == 0)
    def _():
        hs_send(1).wait()
        ig_send(1).wait()

    @pl.when(sec == 1)
    def _():
        hs_send(0).wait()
        ig_send(0).wait()


def body(tokens, cotangent, block_map, gain_a, w_q, w_kv, w_o, gain_f, w_gu, w_d):
    w_kv, w_q = w_kv[0], w_q[0]
    both = jnp.stack([gain_a[0], gain_f[0]], axis=1)
    wq = jnp.concatenate([w_kv[:, :192], w_q, w_kv[:, 192:], both, jnp.zeros((72, 62), BF)], axis=1)
    vm = pl.BlockSpec(memory_space=pltpu.VMEM)
    hs, ig, oq, oo, og, od = pl.pallas_call(
        mega,
        out_shape=(
            jax.ShapeDtypeStruct((2, R, D), BF),
            jax.ShapeDtypeStruct((2, R, D), BF),
            jax.ShapeDtypeStruct((72, 1024), F32),
            jax.ShapeDtypeStruct((72, D), F32),
            jax.ShapeDtypeStruct((72, 2 * FF), F32),
            jax.ShapeDtypeStruct((192, D), F32),
        ),
        in_specs=[vm, vm, pl.BlockSpec(memory_space=pltpu.SMEM), vm, vm, vm, vm],
        out_specs=(vm,) * 6,
        scratch_shapes=[pltpu.VMEM(shape, dtype) for shape, dtype in SCRATCH.values()]
        + [pltpu.SemaphoreType.DMA((N_SEMS,)), pltpu.SemaphoreType.DMA((N_SEMS,))],
        compiler_params=pltpu.CompilerParams(
            collective_id=0, has_side_effects=True, vmem_limit_bytes=64 * 2**20
        ),
        name="layers",
    )(tokens, cotangent, block_map, wq, w_o[0], w_gu[0], w_d[0])
    return (
        hs[None],
        ig[None],
        oq[None, :, 960],
        oq[None, :, 192:768],
        jnp.concatenate([oq[:, :192], oq[:, 768:960]], axis=1)[None],
        oo[None],
        oq[None, :, 961],
        og[None],
        od[None],
    )


def solution(mesh):
    torus = Mesh(mesh.devices.reshape(2, 4, 2, 4, 2), ("section", "z", "ylo", "x", "core"))
    return jax.shard_map(
        body,
        mesh=torus,
        in_specs=(
            P(DP, CONTEXT, None),
            P(DP, CONTEXT, None),
            P(DP, None),
            P("section", DP),
            P("section", DP, None),
            P("section", DP, None),
            P("section", DP, None),
            P("section", DP),
            P("section", DP, None),
            P("section", DP, None),
        ),
        out_specs=(
            P("section", DP, CONTEXT, None),
            P("section", DP, CONTEXT, None),
            P("section", DP),
            P("section", DP, None),
            P("section", DP, None),
            P("section", DP, None),
            P("section", DP),
            P("section", DP, None),
            P("section", DP, None),
        ),
        check_vma=False,
    )
```

time: 895 us -> 253 us (0.28)
  Pallas kernels: 0 us -> 236 us
  blocking collectives: 227 us -> 0 us
  local copies, waits for them, and re-layouts: 215 us -> 13.4 us
  waiting for transfers between devices: 189 us -> 0 us
  matrix products: 127 us -> 0 us
  other arithmetic: 72.9 us -> 0.73 us
  starting transfers between devices: 39.3 us -> 0 us
  between operations: 16.9 us -> 0.7 us
    pallas_call x0 -> x1, Pallas kernels: none -> 236 us  [body(): pl.pallas_call(mega, out_shape=(jax.ShapeDtypeStruct((2, R, D), BF), jax....]
    unnamed x1 -> x0, blocking collectives: 182 us -> none
    dot_general x66 -> x0, matrix products: 127 us -> none  [the longest x3 18.7 us: body(): jnp.einsum('ld,lf->df', normed_ffn, grad_gateup, preferred_element_type=j...]
    all_gather x2 -> x0, waiting for transfers between devices: 125 us -> none  [the longest x1 104 us: side_by_side(): out = lax.all_gather(both, axis, axis=dim, tiled=True)]
    unnamed x314 -> x21, local copies, waits for them, and re-layouts: 102 us -> 7.68 us
    all_gather x3 -> x0, blocking collectives: 45 us -> none  [side_by_side_2(): out = lax.all_gather(both, axis, axis=dim, tiled=True)]
    reduce_scatter x1 -> x0, waiting for transfers between devices: 26.2 us -> none  [summed_rows(): pieces = lax.psum_scatter(pieces, core, scatter_dimension=0, tiled=True)]
    all_to_all x1 -> x0, starting transfers between devices: 25.7 us -> none  [from_everyone(): return lax.all_to_all(copies, axis, split_axis=0, concat_axis=0, tiled=True)]
  transfers between devices with their start and end apart: 11 -> 0, of which waited for: 10 -> 0; matrix products, arithmetic and copies ran while one was open for 14% -> 0% of each run, Pallas kernels for 0% -> 0%
where the time goes in v1:
time: 253 us; the launch traced here: 251 us
  Pallas kernels  236 us (93%)
  local copies, waits for them, and re-layouts  13.4 us (5%)
    pallas_call x1, Pallas kernels, body(): pl.pallas_call(mega, out_shape=(jax.ShapeDtypeStruct((2, R, D), BF), jax....  236 us
    unnamed x21, local copies, waits for them, and re-layouts  7.68 us

profile of v1, /device:TPU:1, one launch (start us, length us, event | category | flops | bytes accessed | tf_op | source)
XLA Modules:
  0.0 250.9 jit_solution(8498232223753150254)
XLA Ops:
  0.6 0.0 copy-start.4
  0.7 0.8 copy.25
  1.5 0.8 copy.26
  2.2 0.9 fusion.1
  3.2 1.7 concatenate.6.wq
  4.9 0.0 copy-done.4
  4.9 0.0 copy-start.5
  4.9 0.9 copy.27.tok
  5.8 0.1 copy-done.5
  5.8 0.9 copy.28.cot
  6.7 236.0 %layers.1 = (bf16[2,128,576]{2,1,0:T(8,128)(2,1)}, bf16[2,128,576]{2,1,0:T(8,128)(2,1)}, f32[72,1024]{1,0:T(8,128)}, f32[72,576]{1,0:T(8,128)}, f32[72,3072]{1,0:T(8,128)}, /*index=5*/f32[192,576]{1,0:T(8,128)}) custom-call(bf16[2,128,576]{2,1,0:T(8,128)(2,1)} %copy.27.tok, bf16[2,128,576]{2,1,0:T(8,128)(2,1)} %copy.28.cot, s32[2,16]{1,0:T(2,128)} %bm.1, ...), custom_call_target="tpu_custom_call" | custom-call | tf_op jit(solution)/shard_map/layers/pallas_call | solution.py:826
  242.8 0.0 copy-start.3
  242.8 0.0 copy-start.1
  242.8 1.9 copy.29
  244.7 0.0 copy-done.3
  244.7 0.0 copy-start
  244.7 0.9 copy.30
  245.6 0.0 copy-done.1
  245.6 0.7 slice_reduce_fusion
  246.3 0.8 slice_bitcast_fusion
  247.1 0.0 copy-start.6
  247.1 0.7 maximum_bitcast_fusion
  247.9 0.2 copy-done.6
  248.0 0.7 copy.34
  248.7 0.0 copy-done
  248.7 0.0 copy-start.2
  248.7 0.9 copy.35
  249.6 0.4 copy-done.2
  250.1 0.8 copy.36
  (2 shorter events, 0.0 us)
Async XLA Ops:
  0.6 4.2 %copy-start.4 = (bf16[2,128,576]{1,2,0:T(8,128)(2,1)S(1)}, bf16[2,128,576]{1,2,0:T(8,128)(2,1)}, u32[]{:S(2)}) copy-start(bf16[2,128,576]{1,2,0:T(8,128)(2,1)} %param.10) | copy-start | bytes 884740
  4.9 1.0 copy-start.5
  242.8 1.9 copy-start.3
  242.8 2.8 %copy-start.1 = (f32[72,1024]{1,0:T(8,128)S(1)}, f32[72,1024]{1,0:T(8,128)}, u32[]{:S(2)}) copy-start(f32[72,1024]{1,0:T(8,128)} %get-tuple-element.17) | copy-start | bytes 884740
  244.7 4.0 %copy-start = (f32[72,3072]{1,0:T(8,128)S(1)}, f32[72,3072]{1,0:T(8,128)}, u32[]{:S(2)}) copy-start(f32[72,3072]{1,0:T(8,128)} %get-tuple-element.19) | copy-start | bytes 2654212
  247.1 0.9 copy-start.6
  248.7 1.4 copy-start.2

commit v2 on v1

--- a/solution.py
+++ b/solution.py
@@ -41,23 +41,22 @@
     Gg=((2, D, 2 * FF), BF),
     Gq=((2, D, 1024), BF),
     Go=((2, D, D), BF),
-    Gd=((2, FF, D), BF),
+    Gd=((2, FF, 640), BF),
     Rg=((D, 2 * FF), BF),
     Rq=((D, 1024), BF),
     Ro=((D, D), BF),
-    Rd=((FF, D), BF),
+    Rd=((FF, 640), BF),
     Sg=((4, 72, 768), BF),
     Sq=((4, 72, 1024), BF),
     So=((4, 72, D), BF),
-    Sd=((4, 192, D), BF),
-    Zg=((3, 144, 768), BF),
     Yg=((3, 72, 768), BF),
     Yq=((3, 72, 1024), BF),
     Yo=((3, 72, D), BF),
-    Yd=((3, 192, D), BF),
+    Yd=((3, 192, 640), BF),
     Xq=((4, 72, 1024), BF),
     Xo=((4, 72, D), BF),
-    Xd=((4, 192, D), BF),
+    Xd=((4, 192, 640), BF),
+    Xg=((4, 72, 768), BF),
     PR=((2, 9, R, 1024), BF),
     GU=((2, R, 2 * FF), BF),
     KV=((2, 1024, 384), BF),
@@ -69,22 +68,22 @@
     MIX=((2, R, D), F32),
     HSB=((2, R, D), BF),
     IGB=((2, R, D), BF),
-    GGU=((R, 2 * FF), BF),
     ACC=((R, D), F32),
     DKV=((8, 384, R), BF),
-    DS=((4, 384, R), BF),
-    DT=((4, 384, R), BF),
-    DX=((2, 3, 384, R), BF),
+    DS=((8, 384, R), BF),
+    DX=((2, 3, 2, 384, R), BF),
+    SND=((384, R), BF),
+    TOT=((384, R), BF),
     COS=((R, R), F32),
     SIN=((R, R), F32),
     BIAS=((R, 1024), F32),
 )
-N_SEMS = 224
+N_SEMS = 256
 
 
 def mega(tok, cot, bm, wq, wo, wg, wd, hs, ig, oq, oo, og, od, *scratch):
     s = dict(zip(SCRATCH, scratch))
-    ss, rs = scratch[-2], scratch[-1]
+    ss, rs, free = scratch[-3:]
     sec = lax.axis_index("section")
     z = lax.axis_index("z")
     ylo = lax.axis_index("ylo")
@@ -138,22 +137,28 @@
     pl.semaphore_wait(barrier, len(peers))
 
     W = dict(q=s["Wq"], o=s["Wo"], d=s["Wd"])
-    S = dict(q=s["Sq"], o=s["So"], d=s["Sd"])
+    S = dict(q=s["Sq"], o=s["So"])
     own = dict(q=wq, o=wo, d=wd)
     OTHERS = ("q", "o", "d")
 
     def ag_y(m, k):
         if m == "g":
             return cp(("ay", m, k), wg.at[:, cols(768, x)], s["Sg"].at[y], at(dy=k))
-        if m == "d":
-            return cp(("ay", m, k), wd, s["Wd"].at[sec, rows(192, d)], at(dy=k))
         return cp(("ay", m, k), own[m], S[m].at[y], at(dy=k))
+
+    def down_z(k):
+        return cp(("dz", k), wd, s["Wd"].at[sec, rows(192, d)], at(dz=k))
+
+    def down_y(k, zz):
+        part = s["Wd"].at[sec, rows(192, 2 * zz + ylo)]
+        return cp(("dy", k, zz), part, part, at(dy=k))
+
+    def from_section(k):
+        return lax.div(lax.rem(y + 4 - k, 4), 2)
 
     def ag_z(m, L, k):
         if m == "g":
             part = s["Wg"].at[L, rows(144, z), cols(768, x)]
-        elif m == "d":
-            part = s["Wd"].at[L, rows(384, z)]
         else:
             part = W[m].at[L, rows(144, z)]
         return cp(("az", m, L, k), part, part, at(dz=k))
@@ -162,6 +167,10 @@
         part = s["Wg"].at[L, :, cols(768, x)]
         return cp(("ax", L, k), part, part, at(dx=k))
 
+    def ag_x2(L, k):
+        part = s["Wg"].at[L, pl.ds(0 if k == 1 else 288, 288), cols(768, lax.rem(x + 4 - k, 4))]
+        return cp(("ax2", L, k), part, part, at(dx=k))
+
     def ag_sib_g(L, k):
         part = s["Wg"].at[L, :, cols(768, lax.rem(x + 4 - k, 4))]
         return cp(("asg", L, k), part, part, at(dc=1))
@@ -172,7 +181,7 @@
 
     def join(m, L):
         buf = s["Sg"] if m == "g" else S[m]
-        both = jnp.concatenate([buf[2 * L].astype(F32), buf[2 * L + 1].astype(F32)], axis=0).astype(BF)
+        both = jnp.concatenate([buf[2 * L + h].astype(F32) for h in (0, 1)], axis=0).astype(BF)
         if m == "g":
             s["Wg"][L, rows(144, z), cols(768, x)] = both
         else:
@@ -180,9 +189,10 @@
 
     @pl.when(is1)
     def _():
-        for m in OTHERS:
-            for k in (1, 2, 3):
-                ag_y(m, k).start()
+        for k in (1, 2, 3):
+            ag_y("q", k).start()
+        for k in (1, 2, 3):
+            down_z(k).start()
         s["Sq"][y] = wq[...]
         s["So"][y] = wo[...]
         s["Wd"][sec, rows(192, d), :] = wd[...]
@@ -193,49 +203,80 @@
             ag_y("g", k).start()
         s["Sg"][y] = wg[:, cols(768, x)]
 
-    lane = lax.broadcasted_iota(jnp.int32, (R, R), 1)
-    row = lax.broadcasted_iota(jnp.int32, (R, R), 0)
-    first = row < 64
-    pos_t = jnp.where(first, bm[sec, 2 * ctx], bm[sec, 2 * ctx + 1]) * 64 + jnp.where(first, row, row - 64)
-    freq = jnp.exp((lane % 32).astype(F32) * F32(-2.0 / 64 * jnp.log(ROPE_BASE)))
-    angle = pos_t.astype(F32) * freq
-    s["COS"][...] = jnp.cos(angle)
-    sine = jnp.sin(angle)
-    s["SIN"][...] = jnp.where(lane % 64 < 32, -sine, sine)
-    pos_f = pos_t[:, :1].astype(F32)
-    for j in range(16):
-        u = lax.broadcasted_iota(jnp.int32, (R, 64), 1) + bm[sec, j] * 64
-        s["BIAS"][:, 64 * j : 64 * j + 64] = jnp.where(u.astype(F32) <= pos_f, 0.0, -1e30).astype(F32)
-
-    def ag_start_z(L):
+    def tables():
+        lane = lax.broadcasted_iota(jnp.int32, (R, R), 1)
+        row = lax.broadcasted_iota(jnp.int32, (R, R), 0)
+        first = row < 64
+        pos_t = jnp.where(first, bm[sec, 2 * ctx], bm[sec, 2 * ctx + 1]) * 64 + jnp.where(first, row, row - 64)
+        freq = jnp.exp((lane % 32).astype(F32) * F32(-2.0 / 64 * jnp.log(ROPE_BASE)))
+        angle = pos_t.astype(F32) * freq
+        s["COS"][...] = jnp.cos(angle)
+        sine = jnp.sin(angle)
+        s["SIN"][...] = jnp.where(lane % 64 < 32, -sine, sine)
+        pos_f = pos_t[:, :1].astype(F32)
+        for j in range(16):
+            u = lax.broadcasted_iota(jnp.int32, (R, 64), 1) + bm[sec, j] * 64
+            s["BIAS"][:, 64 * j : 64 * j + 64] = jnp.where(u.astype(F32) <= pos_f, 0.0, -1e30).astype(F32)
+
+    def ag_start_o():
         @pl.when(is1)
         def _():
-            for m in OTHERS:
-                if L == 0:
-                    for k in (1, 2, 3):
-                        ag_y(m, k).wait_recv()
-                if m != "d":
-                    join(m, L)
+            for k in (1, 2, 3):
+                ag_y("o", k).start()
+
+    def wait_y(m):
+        for k in (1, 2, 3):
+            ag_y(m, k).wait_recv()
+
+    def ag_start_z(m, L):
+        @pl.when(is0 if m == "g" else is1)
+        def _():
+            if L == 0:
+                wait_y(m)
+            join(m, L)
+            if m == "q" and L == 0:
+                pl.semaphore_wait(free.at[3], 1)
+            for k in (1, 2, 3):
+                ag_z(m, L, k).start()
+
+    def down_send(L):
+        @pl.when(is1 & (sec == L))
+        def _():
+            for k in (1, 2, 3):
+                down_z(k).wait_recv()
+            for zz in range(4):
                 for k in (1, 2, 3):
-                    ag_z(m, L, k).start()
-
-        @pl.when(is0)
-        def _():
-            if L == 0:
-                for k in (1, 2, 3):
-                    ag_y("g", k).wait_recv()
-            join("g", L)
-            for k in (1, 2, 3):
-                ag_z("g", L, k).start()
+                    down_y(k, zz).start()
+
+    def down_have(L):
+        @pl.when(is1)
+        def _():
+            for k in (1, 2, 3):
+                @pl.when(from_section(k) == L)
+                def _():
+                    for zz in range(4):
+                        down_y(k, zz).wait_recv()
+            ag_sib("d", L).start()
 
     def ag_fwd_x(L):
         @pl.when(is0)
         def _():
             for k in (1, 2, 3):
                 ag_z("g", L, k).wait_recv()
-            for k in (1, 2, 3):
+            for k in (1, 3):
                 ag_x(L, k).start()
+            if L == 0:
+                pl.semaphore_signal(free.at[3], inc=1, device_id=at(dc=1), device_id_type=MESH)
             ag_sib_g(L, 0).start()
+
+    def ag_fwd_x2(L):
+        @pl.when(is0)
+        def _():
+            for k in (1, 3):
+                ag_x(L, k).wait_recv()
+                ag_x2(L, k).start()
+            for k in (1, 3):
+                ag_sib_g(L, k).start()
 
     def ag_fwd_sib(m, L):
         @pl.when(is1)
@@ -247,9 +288,9 @@
     def ag_fwd_sib_g(L):
         @pl.when(is0)
         def _():
-            for k in (1, 2, 3):
-                ag_x(L, k).wait_recv()
-                ag_sib_g(L, k).start()
+            for k in (1, 3):
+                ag_x2(L, k).wait_recv()
+            ag_sib_g(L, 2).start()
 
     def need(m, L):
         if m == "g":
@@ -265,12 +306,18 @@
     def ag_done():
         @pl.when(is1)
         def _():
+            for k in (1, 2, 3):
+                down_z(k).wait_send()
+                for zz in range(4):
+                    down_y(k, zz).wait_send()
             for m in OTHERS:
-                for k in (1, 2, 3):
-                    ag_y(m, k).wait_send()
+                if m != "d":
+                    for k in (1, 2, 3):
+                        ag_y(m, k).wait_send()
                 for L in (0, 1):
-                    for k in (1, 2, 3):
-                        ag_z(m, L, k).wait_send()
+                    if m != "d":
+                        for k in (1, 2, 3):
+                            ag_z(m, L, k).wait_send()
                     ag_sib(m, L).wait_send()
 
         @pl.when(is0)
@@ -280,7 +327,9 @@
             for L in (0, 1):
                 for k in (1, 2, 3):
                     ag_z("g", L, k).wait_send()
+                for k in (1, 3):
                     ag_x(L, k).wait_send()
+                    ag_x2(L, k).wait_send()
                 for k in (0, 1, 2, 3):
                     ag_sib_g(L, k).wait_send()
 
@@ -301,13 +350,27 @@
         both = mm_tn(s["Wq"][L, :, 896:1024], eye)
         return both[64:65], both[65:66]
 
-    def kv_x(L, k):
+    def kv_up(L):
         part = s["KV"].at[L, rows(R, ctx)]
-        return cp(("kx", L, k), part, part, at(dx=k))
-
-    def kv_sib(L, k):
-        part = s["KV"].at[L, rows(R, lax.rem(x + 4 - k, 4) * 2 + core)]
-        return cp(("ks", L, k), part, part, at(dc=1))
+        return cp(("ku", L), part, part, at(dc=1))
+
+    def kv_x(L, who, k):
+        part = s["KV"].at[L, rows(R, 2 * x + who)]
+        return cp(("kx", L, who, k), part, part, at(dx=k))
+
+    def kv_down(L, k):
+        part = s["KV"].at[L, rows(2 * R, lax.rem(x + 4 - k, 4))]
+        return cp(("kd", L, k), part, part, at(dc=1))
+
+    def kv_done(L):
+        kv_up(L).wait_send()
+
+        @pl.when(is1)
+        def _():
+            for k in (1, 2, 3):
+                for who in (0, 1):
+                    kv_x(L, who, k).wait_send()
+                kv_down(L, k).wait_send()
 
     def hs_send(L):
         return cp("hs", s["HSB"].at[L], hs.at[sec], at(dy=2))
@@ -325,17 +388,34 @@
         kq = qkv[:, :768]
         kq = kq * tiled(s["COS"][...], 6) + swap(kq) * tiled(s["SIN"][...], 6)
         s["KV"][L, rows(R, ctx), :] = jnp.concatenate([kq[:, :192], qkv[:, 768:960]], axis=1).astype(BF)
-        for k in (1, 2, 3):
-            kv_x(L, k).start()
-        kv_sib(L, 0).start()
+        kv_up(L).start()
+
+        @pl.when(is1)
+        def _():
+            for k in (1, 2, 3):
+                kv_x(L, 1, k).start()
+            kv_up(L).wait_recv()
+            for k in (1, 2, 3):
+                kv_x(L, 0, k).start()
+
         s["QS"][L] = (kq[:, 192:768] * 0.125).astype(BF)
         mid[0]()
-        for k in (1, 2, 3):
-            kv_x(L, k).wait_recv()
-            kv_sib(L, k).start()
+
+        @pl.when(is1)
+        def _():
+            for k in (1, 2, 3):
+                for who in (0, 1):
+                    kv_x(L, who, k).wait_recv()
+                kv_down(L, k).start()
+
         mid[1]()
-        for k in (0, 1, 2, 3):
-            kv_sib(L, k).wait_recv()
+
+        @pl.when(is0)
+        def _():
+            kv_up(L).wait_recv()
+            for k in (1, 2, 3):
+                kv_down(L, k).wait_recv()
+
         outs = []
         for kh in range(3):
             keys_h = s["KV"][L, :, 64 * kh : 64 * kh + 64]
@@ -383,12 +463,12 @@
     RAW = dict(q=s["Rq"], o=s["Ro"], d=s["Rd"], g=s["Rg"])
     WALL = dict(W, g=s["Wg"])
     ZN = dict(q=144, o=144, d=384)
-    YR = dict(q=s["Yq"], o=s["Yo"], d=s["Yd"])
+    YR = dict(q=s["Yq"], o=s["Yo"])
     XR = dict(q=s["Xq"], o=s["Xo"], d=s["Xd"])
     OUT = dict(q=oq, o=oo, d=od)
 
     def ra(m, L):
-        return RAW[m] if L == 1 else WALL[m].at[1]
+        return RAW[m] if L == 1 or m in "gd" else WALL[m].at[1]
 
     def rz(m, L):
         return G[m].at[0] if L == 1 else RAW[m]
@@ -396,29 +476,54 @@
     def g_sib(m, L):
         return cp(("gs", m, L), G[m].at[L], ra(m, L), at(dc=1))
 
-    def grad_out(m, L):
+    parts = {(m, L): [sem(("part", m, L, i)) for i in range(4)][0] for m in "gd" for L in (0, 1)}
+
+    def g_part(m, L, i):
+        at_i = (slice(None), cols(768, i)) if m == "g" else (rows(384, i),)
+        j = parts[m, L] + i
+        return pltpu.make_async_remote_copy(
+            src_ref=G[m].at[(L, *at_i)],
+            dst_ref=ra(m, L).at[at_i],
+            send_sem=ss.at[j],
+            recv_sem=rs.at[j],
+            device_id=at(dc=1),
+            device_id_type=MESH,
+        )
+
+    def grad_out(m, L, i=None):
         @pl.when(is1 if m == "g" else is0)
         def _():
-            g_sib(m, L).start()
+            (g_sib(m, L) if i is None else g_part(m, L, i)).start()
 
     def add_sib(m, L):
-        g_sib(m, L).wait_recv()
+        if m not in "gd":
+            g_sib(m, L).wait_recv()
         ref, other = G[m].at[L], ra(m, L)
-        n = ref.shape[0] // 4
 
         @pl.loop(0, 4)
         def _(i):
-            t = rows(n, i)
-            ref[t, :] = (ref[t, :].astype(F32) + other[t, :].astype(F32)).astype(BF)
-
-    def gx(L, k):
-        src = s["Gg"].at[L, :, cols(768, lax.rem(x + k, 4))]
-        dst = (s["Gg"].at[0] if L == 1 else s["Rg"]).at[:, pl.ds(768 * (k - 1), 768)]
-        return cp(("gx", L, k), src, dst, at(dx=k))
+            if m in "gd":
+                g_part(m, L, i).wait_recv()
+            t = (slice(None), cols(768, i)) if m == "g" else (rows(ref.shape[0] // 4, i), slice(None))
+            ref[t] = (ref[t].astype(F32) + other[t].astype(F32)).astype(BF)
+
+    def gx(L, step, k):
+        toward = lax.rem(x + k, 4)
+        top = pl.ds(0, 288)
+        bottom = pl.ds(288, 288)
+        if step == 0:
+            half, col, slot = (top if k == 1 else bottom), lax.rem(x + 2, 4), 0
+        elif step == 1:
+            half, col, slot = (bottom if k == 1 else top), toward, (1 if k == 1 else 2)
+        else:
+            half, col, slot = (top if k == 1 else bottom), toward, (1 if k == 1 else 2)
+        src = s["Gg"].at[L, half, cols(768, col)]
+        dst = s["Wg"].at[1, half, pl.ds(768 * slot, 768)]
+        return cp(("gx", L, step, k), src, dst, at(dx=k))
 
     def gz(L, k):
         src = s["Gg"].at[L, rows(144, lax.rem(z + k, 4)), cols(768, x)]
-        dst = s["Zg"].at[k - 1] if L == 1 else s["Rg"].at[pl.ds(144 * (k - 1), 144), pl.ds(2304, 768)]
+        dst = s["Wg"].at[1, pl.ds(144 * (k - 1), 144), pl.ds(2304, 768)]
         return cp(("gz", L, k), src, dst, at(dz=k))
 
     def y_target(L, k):
@@ -426,39 +531,68 @@
         return lax.div(yy, 2) == L, lax.rem(yy, 2)
 
     def gy(L, k):
-        _, half = y_target(L, k)
-        return cp(("gy", L, k), s["Sg"].at[2 * L + half], s["Yg"].at[k - 1], at(dy=k))
+        _, ours = y_target(L, k)
+        return cp(("gy", L, k), s["Sg"].at[2 * L + ours], s["Yg"].at[k - 1], at(dy=k))
 
     def gfx(L, k):
-        part = og.at[:, cols(768, x)]
-        return cp(("gfx", L, k), part, part, at(dx=k))
+        return cp(("gfx", L, k), s["Xg"].at[x], s["Xg"].at[x], at(dx=k))
 
     def gfs(L, k):
-        part = og.at[:, cols(768, lax.rem(x + 4 - k, 4))]
+        part = s["Xg"].at[lax.rem(x + 4 - k, 4)]
         return cp(("gfs", L, k), part, part, at(dc=1))
+
+    def og_put():
+        for i in range(4):
+            og[:, 768 * i : 768 * i + 768] = s["Xg"][i].astype(F32)
+
+    def give(i, **way):
+        for k in (1, 2, 3):
+            where = at(**{axis: k for axis in way})
+            pl.semaphore_signal(free.at[i], inc=1, device_id=where, device_id_type=MESH)
+
+    def a0(L):
+        @pl.when(is0)
+        def _():
+            add_sib("g", L)
 
     def a1(L):
         @pl.when(is0)
         def _():
-            add_sib("g", L)
-            for k in (1, 2, 3):
-                gx(L, k).start()
+            pl.semaphore_wait(free.at[L], 2)
+            for k in (1, 3):
+                gx(L, 0, k).start()
+
+    def a1b(L):
+        @pl.when(is0)
+        def _():
+            for k in (1, 3):
+                gx(L, 1, k).start()
+            for k in (1, 3):
+                half = pl.ds(0 if k == 1 else 288, 288)
+                at_cols = cols(768, lax.rem(x + k, 4))
+                gx(L, 0, k).wait_recv()
+                both = s["Gg"][L, half, at_cols].astype(F32) + s["Wg"][1, half, :768].astype(F32)
+                s["Gg"][L, half, at_cols] = both.astype(BF)
+                gx(L, 2, k).start()
 
     def a2(L):
         @pl.when(is0)
         def _():
-            for k in (1, 2, 3):
-                gx(L, k).wait_recv()
-            other = s["Gg"].at[0] if L == 1 else s["Rg"]
+            for k in (1, 3):
+                gx(L, 1, k).wait_recv()
+                gx(L, 2, k).wait_recv()
 
             @pl.loop(0, 4)
             def _(i):
                 t = rows(144, i)
                 total = s["Gg"][L, t, cols(768, x)].astype(F32)
-                for k in range(3):
-                    total = total + other[t, 768 * k : 768 * k + 768].astype(F32)
+                for k in (1, 2):
+                    total = total + s["Wg"][1, t, 768 * k : 768 * k + 768].astype(F32)
                 s["Gg"][L, t, cols(768, x)] = total.astype(BF)
 
+            if L == 1:
+                give2(0)
+            pl.semaphore_wait(free.at[4 + L], 3)
             for k in (1, 2, 3):
                 gz(L, k).start()
 
@@ -469,10 +603,11 @@
                 gz(L, k).wait_recv()
             total = s["Gg"][L, rows(144, z), cols(768, x)].astype(F32)
             for k in range(3):
-                other = s["Zg"][k] if L == 1 else s["Rg"][144 * k : 144 * k + 144, 2304:]
-                total = total + other.astype(F32)
+                total = total + s["Wg"][1, 144 * k : 144 * k + 144, 2304:].astype(F32)
             s["Sg"][2 * L] = total[:72].astype(BF)
             s["Sg"][2 * L + 1] = total[72:].astype(BF)
+            if L == 1:
+                give(4, dz=1)
             for k in (1, 2, 3):
                 @pl.when(y_target(L, k)[0])
                 def _():
@@ -486,7 +621,7 @@
             total = s["Sg"][2 * L + ylo].astype(F32)
             for k in range(3):
                 total = total + s["Yg"][k].astype(F32)
-            og[:, cols(768, x)] = total
+            s["Xg"][x] = total.astype(BF)
             for k in (1, 2, 3):
                 gfx(L, k).start()
             gfs(L, 0).start()
@@ -497,6 +632,11 @@
             for k in (1, 2, 3):
                 gfx(L, k).wait_recv()
                 gfs(L, k).start()
+            og_put()
+
+    def give2(i):
+        for k in (1, 3):
+            pl.semaphore_signal(free.at[i], inc=1, device_id=at(dx=k), device_id_type=MESH)
 
     def bz(m, L, k):
         n = ZN[m]
@@ -513,6 +653,55 @@
 
     def bf(m, L):
         return cp(("bf", m, L), OUT[m], OUT[m], at(dc=1))
+
+    def hy(L, k, zz):
+        _, half = y_target(L, k)
+        src = s["Gd"].at[L, rows(192, 2 * zz + half)]
+        dst = s["Wg"].at[1, pl.ds(192 * (k - 1), 192), pl.ds(768 * zz, 640)]
+        return cp(("hy", L, k, zz), src, dst, at(dy=k))
+
+    def hz(L, k):
+        src = s["Gd"].at[L, rows(192, 2 * lax.rem(z + k, 4) + ylo)]
+        return cp(("hz", L, k), src, s["Yd"].at[k - 1], at(dz=k))
+
+    def d1(L):
+        @pl.when(is1)
+        def _():
+            add_sib("d", L)
+            if L == 1:
+                pl.semaphore_wait(free.at[2], 3)
+            for k in (1, 2, 3):
+                @pl.when(y_target(L, k)[0])
+                def _():
+                    for zz in range(4):
+                        hy(L, k, zz).start()
+
+    def d2(L):
+        @pl.when(is1 & (sec == L))
+        def _():
+            for k in (1, 2, 3):
+                for zz in range(4):
+                    hy(L, k, zz).wait_recv()
+            for zz in range(4):
+                t = rows(192, 2 * zz + ylo)
+                total = s["Gd"][L, t, :].astype(F32)
+                for k in range(3):
+                    total = total + s["Wg"][1, 192 * k : 192 * k + 192, 768 * zz : 768 * zz + 640].astype(F32)
+                s["Gd"][L, t, :] = total.astype(BF)
+            for k in (1, 2, 3):
+                hz(L, k).start()
+
+    def d3(L):
+        @pl.when(is1 & (sec == L))
+        def _():
+            for k in (1, 2, 3):
+                hz(L, k).wait_recv()
+            total = s["Gd"][L, rows(192, d), :].astype(F32)
+            for k in range(3):
+                total = total + s["Yd"][k].astype(F32)
+            s["Xd"][x] = total.astype(BF)
+            for k in (1, 2, 3):
+                bx("d", L, k).start()
 
     def b1(m, L):
         @pl.when(is1)
@@ -558,17 +747,21 @@
             total = XR[m][0].astype(F32)
             for k in range(1, 4):
                 total = total + XR[m][k].astype(F32)
-            OUT[m][...] = total
+            OUT[m][...] = total[:, : OUT[m].shape[1]]
             bf(m, L).start()
 
     def grads_done():
         for L in (0, 1):
             @pl.when(is0)
             def _():
-                for m in OTHERS:
+                for i in range(4):
+                    g_part("d", L, i).wait_send()
+                for m in ("q", "o"):
                     g_sib(m, L).wait_send()
+                for k in (1, 3):
+                    for step in range(3):
+                        gx(L, step, k).wait_send()
                 for k in (1, 2, 3):
-                    gx(L, k).wait_send()
                     gz(L, k).wait_send()
 
                     @pl.when(y_target(L, k)[0])
@@ -577,8 +770,14 @@
 
             @pl.when(is1)
             def _():
-                g_sib("g", L).wait_send()
-                for m in OTHERS:
+                for i in range(4):
+                    g_part("g", L, i).wait_send()
+                for k in (1, 2, 3):
+                    @pl.when(y_target(L, k)[0])
+                    def _():
+                        for zz in range(4):
+                            hy(L, k, zz).wait_send()
+                for m in ("q", "o"):
                     for k in (1, 2, 3):
                         bz(m, L, k).wait_send()
 
@@ -597,18 +796,25 @@
 
             @pl.when(is1 & (sec == L))
             def _():
+                for k in (1, 2, 3):
+                    hz(L, k).wait_send()
                 for m in OTHERS:
                     for k in (1, 2, 3):
                         bx(m, L, k).wait_send()
                     bf(m, L).wait_send()
                 for k in range(4):
                     gfs(L, k).wait_recv()
-
-    def dkv_sib(L, j):
-        return cp(("ds", L, j), s["DKV"].at[2 * j + 1 - core], s["DS"].at[j], at(dc=1))
+                og_put()
+
+    def dkv_up(L):
+        return cp(("du", L), s["DKV"], s["DS"], at(dc=1))
 
     def dkv_x(L, k):
-        return cp(("dx", L, k), s["DT"].at[lax.rem(x + k, 4)], s["DX"].at[L, k - 1], at(dx=k))
+        src = s["DKV"].at[pl.ds(2 * lax.rem(x + k, 4), 2)]
+        return cp(("dx", L, k), src, s["DX"].at[L, k - 1], at(dx=k))
+
+    def dkv_down(L):
+        return cp(("dd", L), s["SND"], s["TOT"], at(dc=1))
 
     def backward(L, xin, dF, mid):
         gain_a, gain_f = gains(L)
@@ -623,20 +829,29 @@
             g = s["GU"][L, :, cols(384, q)].astype(F32)
             u = s["GU"][L, :, cols(384, q + 4)].astype(F32)
             sig = 1.0 / (1.0 + jnp.exp(-g))
-            s["GGU"][:, cols(384, q)] = (gh * u * (sig * (1.0 + g * (1.0 - sig)))).astype(BF)
-            s["GGU"][:, cols(384, q + 4)] = (gh * (g * sig)).astype(BF)
-            s["Gd"][L, rows(384, q), :] = mm_tn(s["HID"][L, :, cols(384, q)], up).astype(BF)
-
-        grad_out("d", L)
+            s["GU"][L, :, cols(384, q)] = (gh * u * (sig * (1.0 + g * (1.0 - sig)))).astype(BF)
+            s["GU"][L, :, cols(384, q + 4)] = (gh * (g * sig)).astype(BF)
+            s["Gd"][L, rows(384, q), :D] = mm_tn(s["HID"][L, :, cols(384, q)], up).astype(BF)
+            grad_out("d", L, q)
+
         s["ACC"][...] = jnp.zeros((R, D), F32)
 
         @pl.loop(0, 4)
         def _(q):
-            gg = s["GGU"][:, cols(768, q)]
+            gg = s["GU"][L, :, cols(768, q)]
             s["Gg"][L, :, cols(768, q)] = mm_tn(s["NF"][L], gg).astype(BF)
+            grad_out("g", L, q)
             s["ACC"][...] += mm_nt(gg, s["Wg"][L, :, cols(768, q)])
 
-        grad_out("g", L)
+        if L == 1:
+            @pl.when(is0)
+            def _():
+                give2(1)
+                give(5, dz=1)
+
+            @pl.when(is1)
+            def _():
+                give(2, dy=1)
         gnf = s["ACC"][...]
         mixed = s["MIX"][L]
         r = lax.rsqrt(jnp.mean(mixed * mixed, axis=1, keepdims=True) + EPSILON)
@@ -669,23 +884,41 @@
             for c in range(8):
                 s["DKV"][c, 64 * kh : 64 * kh + 64, :] = dk[:, R * c : R * c + R]
                 s["DKV"][c, 192 + 64 * kh : 256 + 64 * kh, :] = dv[:, R * c : R * c + R]
-        for j in range(4):
-            dkv_sib(L, j).start()
         mid[1]()
-        for j in range(4):
-            dkv_sib(L, j).wait_recv()
-            s["DT"][j] = (s["DKV"][2 * j + core].astype(F32) + s["DS"][j].astype(F32)).astype(BF)
-        for k in (1, 2, 3):
-            dkv_x(L, k).start()
+
+        @pl.when(is0)
+        def _():
+            dkv_up(L).start()
+
+        @pl.when(is1)
+        def _():
+            dkv_up(L).wait_recv()
+            s["DKV"][...] = (s["DKV"][...].astype(F32) + s["DS"][...].astype(F32)).astype(BF)
+            for k in (1, 2, 3):
+                dkv_x(L, k).start()
+
         mid[2]()
-        total = s["DT"][x].astype(F32)
-        for k in (1, 2, 3):
-            dkv_x(L, k).wait_recv()
-            total = total + s["DX"][L, k - 1].astype(F32)
-        for j in range(4):
-            dkv_sib(L, j).wait_send()
-        for k in (1, 2, 3):
-            dkv_x(L, k).wait_send()
+
+        @pl.when(is1)
+        def _():
+            total = s["DKV"][pl.ds(2 * x, 2)].astype(F32)
+            for k in (1, 2, 3):
+                dkv_x(L, k).wait_recv()
+                total = total + s["DX"][L, k - 1].astype(F32)
+            s["SND"][...] = total[0].astype(BF)
+            s["TOT"][...] = total[1].astype(BF)
+            dkv_down(L).start()
+            for k in (1, 2, 3):
+                dkv_x(L, k).wait_send()
+            dkv_down(L).wait_send()
+
+        @pl.when(is0)
+        def _():
+            dkv_down(L).wait_recv()
+            dkv_up(L).wait_send()
+
+        mid[3]()
+        total = s["TOT"][...].astype(F32)
         gkv = total.T
         kq = jnp.concatenate([gkv[:, :192]] + gqs, axis=1)
         kq = kq * tiled(s["COS"][...], 6) - swap(kq) * tiled(s["SIN"][...], 6)
@@ -715,94 +948,104 @@
         def _():
             ig_send(1 if L == 1 else 0).start()
 
-    ag_start_z(0)
+    none = lambda: None
+    ag_start_z("g", 0)
+    down_send(0)
+    ag_start_z("q", 0)
+    ag_start_o()
+    tables()
     ag_fwd_x(0)
     ag_fwd_sib("q", 0)
 
     def f00():
+        ag_start_z("g", 1)
+        ag_start_z("o", 0)
+        ag_start_z("q", 1)
+        ag_fwd_x2(0)
+
+    def f01():
+        ag_start_z("o", 1)
+
+    def f02():
         ag_fwd_sib("o", 0)
-
-    def f01():
-        pass
-
-    def f02():
-        ag_fwd_sib("d", 0)
-        ag_start_z(1)
+        down_have(0)
+        down_send(1)
 
     def f03():
         ag_fwd_sib_g(0)
-
-    def f04():
+        ag_fwd_x(1)
         ag_fwd_sib("q", 1)
-        ag_fwd_x(1)
-
-    forward(0, tok[sec].astype(F32), (f00, f01, f02, f03, f04))
+
+    forward(0, tok[sec].astype(F32), (f00, f01, f02, f03, none))
 
     def f10():
+        ag_fwd_x2(1)
+
+    def f12():
         ag_fwd_sib("o", 1)
-        ag_fwd_sib("d", 1)
 
     def f13():
         ag_fwd_sib_g(1)
-
-    none = lambda: None
-    forward(1, s["HSB"][0].astype(F32), (f10, none, none, f13, none))
+        down_have(1)
+
+    forward(1, s["HSB"][0].astype(F32), (f10, none, f12, f13, none))
     ag_done()
-    for L in (0, 1):
-        for k in (1, 2, 3):
-            kv_x(L, k).wait_send()
-        for k in range(4):
-            kv_sib(L, k).wait_send()
-
-    def c10():
+    kv_done(0)
+    kv_done(1)
+
+    def c11():
+        a0(1)
         a1(1)
-        b1("d", 1)
-
-    def c11():
+        d1(1)
         b1("o", 1)
 
     def c12():
-        b2("d", 1)
-
-    low = backward(1, s["HSB"][0].astype(F32), cot[sec].astype(F32), (c10, c11, c12))
+        a1b(1)
+
+    low = backward(1, s["HSB"][0].astype(F32), cot[sec].astype(F32), (none, c11, c12, none))
     put_ig(1, low)
     b2("o", 1)
-    a2(1)
-    b1("q", 1)
 
     def c00():
+        a2(1)
+        b1("q", 1)
+
+    def c01():
+        a0(0)
+        a1(0)
+        d1(0)
+        b1("o", 0)
+
+    def c02():
+        a1b(0)
+        d2(1)
+        b2("q", 1)
+
+    def c03():
         a3(1)
-        b3("d", 1)
-        b3("o", 1)
-        a1(0)
-        b1("d", 0)
-
-    def c01():
-        b2("q", 1)
-        b1("o", 0)
-        a4(1)
-        b4("d", 1)
-        b4("o", 1)
-
-    def c02():
-        b3("q", 1)
-        a5(1)
-        b2("d", 0)
-
-    low = backward(0, tok[sec].astype(F32), s["IGB"][1].astype(F32), (c00, c01, c02))
+
+    low = backward(0, tok[sec].astype(F32), s["IGB"][1].astype(F32), (c00, c01, c02, c03))
     put_ig(0, low)
-    b4("q", 1)
     b1("q", 0)
+    d2(0)
     b2("o", 0)
     a2(0)
+    a4(1)
+    d3(1)
+    b3("o", 1)
+    b3("q", 1)
     b2("q", 0)
-    b3("d", 0)
+    a3(0)
+    d3(0)
     b3("o", 0)
-    a3(0)
     b3("q", 0)
+    a5(1)
+    b4("d", 1)
+    b4("o", 1)
+    b4("q", 1)
+    a4(0)
     b4("d", 0)
     b4("o", 0)
-    a4(0)
     b4("q", 0)
     a5(0)
     grads_done()
@@ -836,7 +1079,8 @@
         in_specs=[vm, vm, pl.BlockSpec(memory_space=pltpu.SMEM), vm, vm, vm, vm],
         out_specs=(vm,) * 6,
         scratch_shapes=[pltpu.VMEM(shape, dtype) for shape, dtype in SCRATCH.values()]
-        + [pltpu.SemaphoreType.DMA((N_SEMS,)), pltpu.SemaphoreType.DMA((N_SEMS,))],
+        + [pltpu.SemaphoreType.DMA((N_SEMS,))] * 2
+        + [pltpu.SemaphoreType.REGULAR((6,))],
         compiler_params=pltpu.CompilerParams(
             collective_id=0, has_side_effects=True, vmem_limit_bytes=64 * 2**20
         ),

time: 253 us -> 192 us (0.76)
  Pallas kernels: 236 us -> 177 us
    pallas_call x1, Pallas kernels: 236 us -> 177 us  [body(): pl.pallas_call(mega, out_shape=(jax.ShapeDtypeStruct((2, R, D), BF), jax....]
where the time goes in v2:
time: 192 us
  Pallas kernels  177 us (92%)
  local copies, waits for them, and re-layouts  13.4 us (7%)
    pallas_call x1, Pallas kernels, body(): pl.pallas_call(mega, out_shape=(jax.ShapeDtypeStruct((2, R, D), BF), jax....  177 us
    unnamed x21, local copies, waits for them, and re-layouts  7.68 us

profile of v2, /device:TPU:1, one launch (start us, length us, event | category | flops | bytes accessed | tf_op | source)
XLA Modules:
  0.0 191.6 jit_solution(10439919697353763311)
XLA Ops:
  0.6 0.0 copy-start.4
  0.7 0.8 copy.25
  1.5 0.8 copy.26
  2.2 0.9 fusion.1
  3.2 1.7 concatenate.6.wq
  4.9 0.0 copy-done.4
  4.9 0.0 copy-start.5
  4.9 0.9 copy.27.tok
  5.8 0.1 copy-done.5
  5.8 0.9 copy.28.cot
  6.7 176.8 %layers.1 = (bf16[2,128,576]{2,1,0:T(8,128)(2,1)}, bf16[2,128,576]{2,1,0:T(8,128)(2,1)}, f32[72,1024]{1,0:T(8,128)}, f32[72,576]{1,0:T(8,128)}, f32[72,3072]{1,0:T(8,128)}, /*index=5*/f32[192,576]{1,0:T(8,128)}) custom-call(bf16[2,128,576]{2,1,0:T(8,128)(2,1)} %copy.27.tok, bf16[2,128,576]{2,1,0:T(8,128)(2,1)} %copy.28.cot, s32[2,16]{1,0:T(2,128)} %bm.1, ...), custom_call_target="tpu_custom_call" | custom-call | tf_op jit(solution)/shard_map/layers/pallas_call | solution.py:1069
  183.6 0.0 copy-start.3
  183.6 0.0 copy-start.1
  183.6 1.9 %copy.29 = bf16[1,2,128,576]{2,3,1,0:T(8,128)(2,1)} copy(bf16[1,2,128,576]{3,2,1,0:T(8,128)(2,1)} %bitcast.22) | data formatting | bytes 589824
  185.5 0.0 copy-done.3
  185.5 0.0 copy-start
  185.5 0.9 copy.30
  186.4 0.0 copy-done.1
  186.4 0.7 slice_reduce_fusion
  187.1 0.8 slice_bitcast_fusion
  187.9 0.0 copy-start.6
  187.9 0.7 maximum_bitcast_fusion
  188.6 0.2 copy-done.6
  188.8 0.7 copy.34
  189.5 0.0 copy-done
  189.5 0.0 copy-start.2
  189.5 0.9 copy.35
  190.4 0.4 copy-done.2
  190.9 0.8 copy.36
  (2 shorter events, 0.0 us)
Async XLA Ops:
  0.6 4.2 %copy-start.4 = (bf16[2,128,576]{1,2,0:T(8,128)(2,1)S(1)}, bf16[2,128,576]{1,2,0:T(8,128)(2,1)}, u32[]{:S(2)}) copy-start(bf16[2,128,576]{1,2,0:T(8,128)(2,1)} %param.10) | copy-start | bytes 884740
  4.9 1.0 copy-start.5
  183.6 1.9 %copy-start.3 = (bf16[2,128,576]{2,1,0:T(8,128)(2,1)S(1)}, bf16[2,128,576]{2,1,0:T(8,128)(2,1)}, u32[]{:S(2)}) copy-start(bf16[2,128,576]{2,1,0:T(8,128)(2,1)} %get-tuple-element.16) | copy-start | bytes 884740
  183.6 2.8 %copy-start.1 = (f32[72,1024]{1,0:T(8,128)S(1)}, f32[72,1024]{1,0:T(8,128)}, u32[]{:S(2)}) copy-start(f32[72,1024]{1,0:T(8,128)} %get-tuple-element.17) | copy-start | bytes 884740
  185.5 4.0 %copy-start = (f32[72,3072]{1,0:T(8,128)S(1)}, f32[72,3072]{1,0:T(8,128)}, u32[]{:S(2)}) copy-start(f32[72,3072]{1,0:T(8,128)} %get-tuple-element.19) | copy-start | bytes 2654212
  187.9 0.9 copy-start.6
  189.5 1.4 copy-start.2

commit v3 on v2

--- a/solution.py
+++ b/solution.py
@@ -66,8 +66,8 @@
     ATT=((2, R, D), BF),
     QS=((2, R, D), BF),
     MIX=((2, R, D), F32),
-    HSB=((2, R, D), BF),
-    IGB=((2, R, D), BF),
+    HSB=((R, D), BF),
+    IGB=((R, D), BF),
     ACC=((R, D), F32),
     DKV=((8, 384, R), BF),
     DS=((8, 384, R), BF),
@@ -77,13 +77,30 @@
     COS=((R, R), F32),
     SIN=((R, R), F32),
     BIAS=((R, 1024), F32),
+    TOK=((R, D), BF),
+    TOKT=((D, R), BF),
+    COTT=((D, R), BF),
+    HST=((D, R), BF),
+    HST1=((D, R), BF),
+    IGT=((D, R), BF),
+    IGT1=((D, R), BF),
+    IQ=((72, D), BF),
+    IKV=((72, 384), BF),
+    VG=((72, 2 * FF), F32),
+    VD=((192, D), F32),
+    VO=((72, D), F32),
+    VQ=((72, 1024), F32),
+    VQ2=((72, D), F32),
+    VKV=((72, 384), F32),
+    VGA=((1, 72), F32),
+    VGF=((1, 72), F32),
 )
 N_SEMS = 256
 
 
-def mega(tok, cot, bm, wq, wo, wg, wd, hs, ig, oq, oo, og, od, *scratch):
+def mega(tok, cot, bm, gain_a, gain_f, wq, wkv, wo, wg, wd, hs, ig, o_ga, o_q, o_kv, o_o, o_gf, o_g, o_d, *scratch):
     s = dict(zip(SCRATCH, scratch))
-    ss, rs, free = scratch[-3:]
+    ss, rs, free, ls = scratch[-4:]
     sec = lax.axis_index("section")
     z = lax.axis_index("z")
     ylo = lax.axis_index("ylo")
@@ -129,6 +146,45 @@
     def cols(n, i):
         return pl.ds(pl.multiple_of(n * i, 128), n)
 
+    def here(i, src, dst):
+        return pltpu.make_async_copy(src, dst, ls.at[i])
+
+    load = dict(
+        tok=here(0, tok.at[sec], s["TOKT"]),
+        cot=here(1, cot.at[sec], s["COTT"]),
+        q=here(2, wq.at[0], s["IQ"]),
+        kv=here(3, wkv.at[0], s["IKV"]),
+        o=here(4, wo.at[0], s["So"].at[y]),
+        d=here(5, wd.at[0], s["Wd"].at[sec, rows(192, d)]),
+        g=here(6, wg.at[0, :, cols(768, x)], s["Sg"].at[y]),
+    )
+    store = dict(
+        g=here(7, s["VG"], o_g.at[0]),
+        d=here(8, s["VD"], o_d.at[0]),
+        o=here(9, s["VO"], o_o.at[0]),
+        q=here(10, s["VQ2"], o_q.at[0]),
+        kv=here(11, s["VKV"], o_kv.at[0]),
+        ga=here(12, s["VGA"], o_ga),
+        gf=here(13, s["VGF"], o_gf),
+        hs0=here(14, s["HST"], hs.at[0, sec]),
+        hs1=here(14, s["HST1"], hs.at[0, sec]),
+        ig0=here(15, s["IGT"], ig.at[0, sec]),
+        ig1=here(15, s["IGT1"], ig.at[0, sec]),
+    )
+
+    load["tok"].start()
+
+    @pl.when(is1)
+    def _():
+        for m in ("q", "kv", "d", "o"):
+            load[m].start()
+
+    @pl.when(is0)
+    def _():
+        load["g"].start()
+
+    load["cot"].start()
+
     barrier = pltpu.get_barrier_semaphore()
     peers = [at(dy=k) for k in (1, 2, 3)] + [at(dz=k) for k in (1, 2, 3)]
     peers += [at(dx=k) for k in (1, 2, 3)] + [at(dc=1)]
@@ -138,16 +194,16 @@
 
     W = dict(q=s["Wq"], o=s["Wo"], d=s["Wd"])
     S = dict(q=s["Sq"], o=s["So"])
-    own = dict(q=wq, o=wo, d=wd)
+    own = dict(q=s["Sq"].at[y], o=wo.at[0])
     OTHERS = ("q", "o", "d")
 
     def ag_y(m, k):
         if m == "g":
-            return cp(("ay", m, k), wg.at[:, cols(768, x)], s["Sg"].at[y], at(dy=k))
+            return cp(("ay", m, k), wg.at[0, :, cols(768, x)], s["Sg"].at[y], at(dy=k))
         return cp(("ay", m, k), own[m], S[m].at[y], at(dy=k))
 
     def down_z(k):
-        return cp(("dz", k), wd, s["Wd"].at[sec, rows(192, d)], at(dz=k))
+        return cp(("dz", k), wd.at[0], s["Wd"].at[sec, rows(192, d)], at(dz=k))
 
     def down_y(k, zz):
         part = s["Wd"].at[sec, rows(192, 2 * zz + ylo)]
@@ -187,21 +243,27 @@
         else:
             W[m][L, rows(144, z), :] = both
 
+    @pl.when(is0)
+    def _():
+        for k in (1, 2, 3):
+            ag_y("g", k).start()
+        load["g"].wait()
+
     @pl.when(is1)
     def _():
+        eye = lax.broadcasted_iota(jnp.int32, (72, 72), 0) == lax.broadcasted_iota(jnp.int32, (72, 72), 1)
+        gain = [jnp.sum(jnp.where(eye, g[...].astype(F32), 0.0), axis=1, keepdims=True) for g in (gain_a, gain_f)]
+        load["q"].wait()
+        load["kv"].wait()
+        kv = s["IKV"][...].astype(F32)
+        parts = [kv[:, :192], s["IQ"][...].astype(F32), kv[:, 192:], *gain, jnp.zeros((72, 62), F32)]
+        s["Sq"][y] = jnp.concatenate(parts, axis=1).astype(BF)
         for k in (1, 2, 3):
             ag_y("q", k).start()
         for k in (1, 2, 3):
             down_z(k).start()
-        s["Sq"][y] = wq[...]
-        s["So"][y] = wo[...]
-        s["Wd"][sec, rows(192, d), :] = wd[...]
-
-    @pl.when(is0)
-    def _():
-        for k in (1, 2, 3):
-            ag_y("g", k).start()
-        s["Sg"][y] = wg[:, cols(768, x)]
+        load["d"].wait()
+        load["o"].wait()
 
     def tables():
         lane = lax.broadcasted_iota(jnp.int32, (R, R), 1)
@@ -234,8 +296,6 @@
             if L == 0:
                 wait_y(m)
             join(m, L)
-            if m == "q" and L == 0:
-                pl.semaphore_wait(free.at[3], 1)
             for k in (1, 2, 3):
                 ag_z(m, L, k).start()
 
@@ -265,8 +325,6 @@
                 ag_z("g", L, k).wait_recv()
             for k in (1, 3):
                 ag_x(L, k).start()
-            if L == 0:
-                pl.semaphore_signal(free.at[3], inc=1, device_id=at(dc=1), device_id_type=MESH)
             ag_sib_g(L, 0).start()
 
     def ag_fwd_x2(L):
@@ -373,10 +431,10 @@
                 kv_down(L, k).wait_send()
 
     def hs_send(L):
-        return cp("hs", s["HSB"].at[L], hs.at[sec], at(dy=2))
+        return cp("hs", s["HST1" if L == 1 else "HST"], hs.at[0, sec], at(dy=2))
 
     def ig_send(L):
-        return cp("ig", s["IGB"].at[L], ig.at[sec], at(dy=2))
+        return cp("ig", s["IGT1" if L == 1 else "IGT"], ig.at[0, sec], at(dy=2))
 
     def forward(L, xin, mid):
         need("q", L)
@@ -416,6 +474,7 @@
             for k in (1, 2, 3):
                 kv_down(L, k).wait_recv()
 
+        mid[5]()
         outs = []
         for kh in range(3):
             keys_h = s["KV"][L, :, 64 * kh : 64 * kh + 64]
@@ -449,11 +508,13 @@
         mid[4]()
         need("d", L)
         out = (s["MIX"][L] + mm(s["HID"][L], s["Wd"][L])).astype(BF)
-        s["HSB"][L] = out
+        if L == 0:
+            s["HSB"][...] = out
+        s["HST1" if L == 1 else "HST"][...] = out.astype(F32).T.astype(BF)
 
         @pl.when(sec == L)
         def _():
-            hs[sec] = out
+            store["hs%d" % L].start()
 
         @pl.when(sec != L)
         def _():
@@ -465,7 +526,7 @@
     ZN = dict(q=144, o=144, d=384)
     YR = dict(q=s["Yq"], o=s["Yo"])
     XR = dict(q=s["Xq"], o=s["Xo"], d=s["Xd"])
-    OUT = dict(q=oq, o=oo, d=od)
+    OUT = dict(q=s["VQ"], o=s["VO"], d=s["VD"])
 
     def ra(m, L):
         return RAW[m] if L == 1 or m in "gd" else WALL[m].at[1]
@@ -543,7 +604,21 @@
 
     def og_put():
         for i in range(4):
-            og[:, 768 * i : 768 * i + 768] = s["Xg"][i].astype(F32)
+            s["VG"][:, 768 * i : 768 * i + 768] = s["Xg"][i].astype(F32)
+        store["g"].start()
+
+    def put(m):
+        if m != "q":
+            store[m].start()
+            return
+        every = s["VQ"][...]
+        s["VQ2"][...] = every[:, 192:768]
+        s["VKV"][...] = jnp.concatenate([every[:, :192], every[:, 768:960]], axis=1)
+        eye = lax.broadcasted_iota(jnp.int32, (72, 72), 0) == lax.broadcasted_iota(jnp.int32, (72, 72), 1)
+        s["VGA"][...] = jnp.sum(jnp.where(eye, every[:, 960:961], 0.0), axis=0, keepdims=True)
+        s["VGF"][...] = jnp.sum(jnp.where(eye, every[:, 961:962], 0.0), axis=0, keepdims=True)
+        for each in ("q", "kv", "ga", "gf"):
+            store[each].start()
 
     def give(i, **way):
         for k in (1, 2, 3):
@@ -749,6 +824,7 @@
                 total = total + XR[m][k].astype(F32)
             OUT[m][...] = total[:, : OUT[m].shape[1]]
             bf(m, L).start()
+            put(m)
 
     def grads_done():
         for L in (0, 1):
@@ -791,8 +867,9 @@
                     gfx(L, k).wait_send()
                 for k in range(4):
                     gfs(L, k).wait_send()
-                for m in OTHERS:
+                for m in ("d", "o", "q"):
                     bf(m, L).wait_recv()
+                    put(m)
 
             @pl.when(is1 & (sec == L))
             def _():
@@ -820,11 +897,11 @@
         gain_a, gain_f = gains(L)
         dlow = dF.astype(BF)
         if L == 1:
-            s["IGB"][1] = dlow
+            s["IGB"][...] = dlow
 
         @pl.loop(0, 4)
         def _(q):
-            up = s["IGB"][1]
+            up = s["IGB"][...]
             gh = mm_nt(up, s["Wd"][L, rows(384, q), :])
             g = s["GU"][L, :, cols(384, q)].astype(F32)
             u = s["GU"][L, :, cols(384, q + 4)].astype(F32)
@@ -938,11 +1015,13 @@
         return low
 
     def put_ig(L, low):
-        s["IGB"][1 if L == 1 else 0] = low
+        if L == 1:
+            s["IGB"][...] = low
+        s["IGT1" if L == 1 else "IGT"][...] = low.astype(F32).T.astype(BF)
 
         @pl.when(sec == L)
         def _():
-            ig[sec] = low
+            store["ig%d" % L].start()
 
         @pl.when(sec != L)
         def _():
@@ -971,12 +1050,16 @@
         down_have(0)
         down_send(1)
 
+    def f05():
+        ag_fwd_x(1)
+
     def f03():
         ag_fwd_sib_g(0)
-        ag_fwd_x(1)
         ag_fwd_sib("q", 1)
 
-    forward(0, tok[sec].astype(F32), (f00, f01, f02, f03, none))
+    load["tok"].wait()
+    s["TOK"][...] = s["TOKT"][...].astype(F32).T.astype(BF)
+    forward(0, s["TOK"][...].astype(F32), (f00, f01, f02, f03, none, f05))
 
     def f10():
         ag_fwd_x2(1)
@@ -988,7 +1071,7 @@
         ag_fwd_sib_g(1)
         down_have(1)
 
-    forward(1, s["HSB"][0].astype(F32), (f10, none, f12, f13, none))
+    forward(1, s["HSB"][...].astype(F32), (f10, none, f12, f13, none, none))
     ag_done()
     kv_done(0)
     kv_done(1)
@@ -1002,101 +1085,123 @@
     def c12():
         a1b(1)
 
-    low = backward(1, s["HSB"][0].astype(F32), cot[sec].astype(F32), (none, c11, c12, none))
+    load["cot"].wait()
+    low = backward(1, s["HSB"][...].astype(F32), s["COTT"][...].astype(F32).T, (none, c11, c12, none))
     put_ig(1, low)
     b2("o", 1)
 
     def c00():
         a2(1)
-        b1("q", 1)
-
-    def c01():
         a0(0)
         a1(0)
         d1(0)
+        b1("q", 1)
+
+    def c01():
         b1("o", 0)
 
     def c02():
         a1b(0)
         d2(1)
-        b2("q", 1)
 
     def c03():
         a3(1)
-
-    low = backward(0, tok[sec].astype(F32), s["IGB"][1].astype(F32), (c00, c01, c02, c03))
+        b2("q", 1)
+        b2("o", 0)
+
+    low = backward(0, s["TOK"][...].astype(F32), s["IGB"][...].astype(F32), (c00, c01, c02, c03))
     put_ig(0, low)
     b1("q", 0)
-    d2(0)
-    b2("o", 0)
     a2(0)
     a4(1)
     d3(1)
     b3("o", 1)
     b3("q", 1)
+    b3("o", 0)
+    d2(0)
     b2("q", 0)
     a3(0)
     d3(0)
-    b3("o", 0)
     b3("q", 0)
     a5(1)
-    b4("d", 1)
     b4("o", 1)
     b4("q", 1)
+    b4("d", 1)
     a4(0)
+    b4("o", 0)
     b4("d", 0)
-    b4("o", 0)
     b4("q", 0)
     a5(0)
     grads_done()
 
+    for m in ("g", "d", "o", "q", "kv", "ga", "gf"):
+        store[m].wait()
+
     @pl.when(sec == 0)
     def _():
+        store["hs0"].wait()
+        store["ig0"].wait()
         hs_send(1).wait()
         ig_send(1).wait()
 
     @pl.when(sec == 1)
     def _():
+        store["hs1"].wait()
+        store["ig1"].wait()
         hs_send(0).wait()
         ig_send(0).wait()
 
 
+def hand_on(*refs):
+    n = 9
+    sems = refs[-1]
+    into = [pltpu.make_async_copy(refs[i], refs[2 * n + i], sems.at[0, i]) for i in range(n)]
+    out = [pltpu.make_async_copy(refs[2 * n + i], refs[n + i], sems.at[1, i]) for i in range(n)]
+    for copy in into:
+        copy.start()
+    for i in range(n):
+        into[i].wait()
+        out[i].start()
+    for copy in out:
+        copy.wait()
+
+
 def body(tokens, cotangent, block_map, gain_a, w_q, w_kv, w_o, gain_f, w_gu, w_d):
-    w_kv, w_q = w_kv[0], w_q[0]
-    both = jnp.stack([gain_a[0], gain_f[0]], axis=1)
-    wq = jnp.concatenate([w_kv[:, :192], w_q, w_kv[:, 192:], both, jnp.zeros((72, 62), BF)], axis=1)
+    any_ = pl.BlockSpec(memory_space=pl.ANY)
     vm = pl.BlockSpec(memory_space=pltpu.VMEM)
-    hs, ig, oq, oo, og, od = pl.pallas_call(
+    shapes = (
+        jax.ShapeDtypeStruct((1, 2, D, R), BF),
+        jax.ShapeDtypeStruct((1, 2, D, R), BF),
+        jax.ShapeDtypeStruct((1, 72), F32),
+        jax.ShapeDtypeStruct((1, 72, D), F32),
+        jax.ShapeDtypeStruct((1, 72, 384), F32),
+        jax.ShapeDtypeStruct((1, 72, D), F32),
+        jax.ShapeDtypeStruct((1, 72), F32),
+        jax.ShapeDtypeStruct((1, 72, 2 * FF), F32),
+        jax.ShapeDtypeStruct((1, 192, D), F32),
+    )
+    outs = pl.pallas_call(
         mega,
-        out_shape=(
-            jax.ShapeDtypeStruct((2, R, D), BF),
-            jax.ShapeDtypeStruct((2, R, D), BF),
-            jax.ShapeDtypeStruct((72, 1024), F32),
-            jax.ShapeDtypeStruct((72, D), F32),
-            jax.ShapeDtypeStruct((72, 2 * FF), F32),
-            jax.ShapeDtypeStruct((192, D), F32),
-        ),
-        in_specs=[vm, vm, pl.BlockSpec(memory_space=pltpu.SMEM), vm, vm, vm, vm],
-        out_specs=(vm,) * 6,
+        out_shape=shapes,
+        in_specs=[any_, any_, pl.BlockSpec(memory_space=pltpu.SMEM), vm, vm] + [any_] * 5,
+        out_specs=(any_,) * 9,
         scratch_shapes=[pltpu.VMEM(shape, dtype) for shape, dtype in SCRATCH.values()]
         + [pltpu.SemaphoreType.DMA((N_SEMS,))] * 2
-        + [pltpu.SemaphoreType.REGULAR((6,))],
+        + [pltpu.SemaphoreType.REGULAR((6,)), pltpu.SemaphoreType.DMA((16,))],
         compiler_params=pltpu.CompilerParams(
             collective_id=0, has_side_effects=True, vmem_limit_bytes=64 * 2**20
         ),
         name="layers",
-    )(tokens, cotangent, block_map, wq, w_o[0], w_gu[0], w_d[0])
-    return (
-        hs[None],
-        ig[None],
-        oq[None, :, 960],
-        oq[None, :, 192:768],
-        jnp.concatenate([oq[:, :192], oq[:, 768:960]], axis=1)[None],
-        oo[None],
-        oq[None, :, 961],
-        og[None],
-        od[None],
-    )
+    )(tokens.swapaxes(1, 2), cotangent.swapaxes(1, 2), block_map, gain_a, gain_f, w_q, w_kv, w_o, w_gu, w_d)
+    hs, ig, *grads = pl.pallas_call(
+        hand_on,
+        out_shape=shapes,
+        in_specs=[any_] * 9,
+        out_specs=(any_,) * 9,
+        scratch_shapes=[pltpu.VMEM(a.shape, a.dtype) for a in shapes] + [pltpu.SemaphoreType.DMA((2, 9))],
+        name="results",
+    )(*outs)
+    return (hs.swapaxes(2, 3), ig.swapaxes(2, 3), *grads)
 
 
 def solution(mesh):

time: 192 us -> 178 us (0.927)
  local copies, waits for them, and re-layouts: 13.4 us -> 0 us
    unnamed x21 -> x0, local copies, waits for them, and re-layouts: 7.68 us -> none
    pallas_call x1 -> x2, Pallas kernels: 177 us -> 176 us  [the longest x1 174 us: body(): pl.pallas_call(mega, out_shape=shapes, in_specs=[any_, any_, pl.BlockSpec...]
where the time goes in v3:
time: 178 us; the launch traced here: 177 us
  Pallas kernels  176 us (99%)
    pallas_call x1, Pallas kernels, body(): pl.pallas_call(mega, out_shape=shapes, in_specs=[any_, any_, pl.BlockSpec...  174 us

profile of v3, /device:TPU:1, one launch (start us, length us, event | category | flops | bytes accessed | tf_op | source)
XLA Modules:
  0.0 177.4 jit_solution(9457886376878137718)
XLA Ops:
  0.6 173.8 %layers.1 = (bf16[1,2,576,128]{3,2,1,0:T(8,128)(2,1)}, bf16[1,2,576,128]{3,2,1,0:T(8,128)(2,1)}, f32[1,72]{1,0:T(1,128)}, f32[1,72,576]{2,1,0:T(8,128)}, f32[1,7...) custom-call(bf16[2,576,128]{2,1,0:T(8,128)(2,1)} %bitcast.4, ...), custom_call_target="tpu_custom_call" | custom-call | tf_op jit(solution)/shard_map/layers/pallas_call | solution.py:1183
  174.4 2.7 %results.1 = (bf16[1,2,576,128]{3,2,1,0:T(8,128)(2,1)}, bf16[1,2,576,128]{3,2,1,0:T(8,128)(2,1)}, f32[1,72]{1,0:T(1,128)}, f32[1,72,576]{2,1,0:T(8,128)}, f32[1,...) custom-call(bf16[1,2,576,128]{3,2,1,0:T(8,128)(2,1)} %get-tuple-elem, ...), custom_call_target="tpu_custom_call" | custom-call | tf_op jit(solution)/shard_map/results/pallas_call | solution.py:1196

commit v4 on v3

--- a/solution.py
+++ b/solution.py
@@ -74,6 +74,7 @@
     DX=((2, 3, 2, 384, R), BF),
     SND=((384, R), BF),
     TOT=((384, R), BF),
+    GN=((2, 8, D), F32),
     COS=((R, R), F32),
     SIN=((R, R), F32),
     BIAS=((R, 1024), F32),
@@ -245,7 +246,7 @@
 
     @pl.when(is0)
     def _():
-        for k in (1, 2, 3):
+        for k in (2, 1, 3):
             ag_y("g", k).start()
         load["g"].wait()
 
@@ -258,9 +259,9 @@
         kv = s["IKV"][...].astype(F32)
         parts = [kv[:, :192], s["IQ"][...].astype(F32), kv[:, 192:], *gain, jnp.zeros((72, 62), F32)]
         s["Sq"][y] = jnp.concatenate(parts, axis=1).astype(BF)
-        for k in (1, 2, 3):
+        for k in (2, 1, 3):
             ag_y("q", k).start()
-        for k in (1, 2, 3):
+        for k in (2, 1, 3):
             down_z(k).start()
         load["d"].wait()
         load["o"].wait()
@@ -283,7 +284,7 @@
     def ag_start_o():
         @pl.when(is1)
         def _():
-            for k in (1, 2, 3):
+            for k in (2, 1, 3):
                 ag_y("o", k).start()
 
     def wait_y(m):
@@ -296,7 +297,7 @@
             if L == 0:
                 wait_y(m)
             join(m, L)
-            for k in (1, 2, 3):
+            for k in (2, 1, 3):
                 ag_z(m, L, k).start()
 
     def down_send(L):
@@ -305,7 +306,7 @@
             for k in (1, 2, 3):
                 down_z(k).wait_recv()
             for zz in range(4):
-                for k in (1, 2, 3):
+                for k in (2, 1, 3):
                     down_y(k, zz).start()
 
     def down_have(L):
@@ -406,6 +407,7 @@
             lax.broadcasted_iota(jnp.int32, (D, D), 0) == lax.broadcasted_iota(jnp.int32, (D, D), 1)
         ).astype(F32).astype(BF)
         both = mm_tn(s["Wq"][L, :, 896:1024], eye)
+        s["GN"][L] = both[64:72]
         return both[64:65], both[65:66]
 
     def kv_up(L):
@@ -453,7 +455,7 @@
             for k in (1, 2, 3):
                 kv_x(L, 1, k).start()
             kv_up(L).wait_recv()
-            for k in (1, 2, 3):
+            for k in (2, 1, 3):
                 kv_x(L, 0, k).start()
 
         s["QS"][L] = (kq[:, 192:768] * 0.125).astype(BF)
@@ -668,7 +670,7 @@
             if L == 1:
                 give2(0)
             pl.semaphore_wait(free.at[4 + L], 3)
-            for k in (1, 2, 3):
+            for k in (2, 1, 3):
                 gz(L, k).start()
 
     def a3(L):
@@ -683,7 +685,7 @@
             s["Sg"][2 * L + 1] = total[72:].astype(BF)
             if L == 1:
                 give(4, dz=1)
-            for k in (1, 2, 3):
+            for k in (2, 1, 3):
                 @pl.when(y_target(L, k)[0])
                 def _():
                     gy(L, k).start()
@@ -697,7 +699,7 @@
             for k in range(3):
                 total = total + s["Yg"][k].astype(F32)
             s["Xg"][x] = total.astype(BF)
-            for k in (1, 2, 3):
+            for k in (2, 1, 3):
                 gfx(L, k).start()
             gfs(L, 0).start()
 
@@ -763,7 +765,7 @@
                 for k in range(3):
                     total = total + s["Wg"][1, 192 * k : 192 * k + 192, 768 * zz : 768 * zz + 640].astype(F32)
                 s["Gd"][L, t, :] = total.astype(BF)
-            for k in (1, 2, 3):
+            for k in (2, 1, 3):
                 hz(L, k).start()
 
     def d3(L):
@@ -775,14 +777,14 @@
             for k in range(3):
                 total = total + s["Yd"][k].astype(F32)
             s["Xd"][x] = total.astype(BF)
-            for k in (1, 2, 3):
+            for k in (2, 1, 3):
                 bx("d", L, k).start()
 
     def b1(m, L):
         @pl.when(is1)
         def _():
             add_sib(m, L)
-            for k in (1, 2, 3):
+            for k in (2, 1, 3):
                 bz(m, L, k).start()
 
     def b2(m, L):
@@ -797,7 +799,7 @@
                 total = total + rz(m, L)[n * k : n * k + n, :].astype(F32)
             S[m][2 * L] = total[: n // 2].astype(BF)
             S[m][2 * L + 1] = total[n // 2 :].astype(BF)
-            for k in (1, 2, 3):
+            for k in (2, 1, 3):
                 @pl.when(y_target(L, k)[0])
                 def _():
                     by(m, L, k).start()
@@ -811,7 +813,7 @@
             for k in range(3):
                 total = total + YR[m][k].astype(F32)
             XR[m][x] = total.astype(BF)
-            for k in (1, 2, 3):
+            for k in (2, 1, 3):
                 bx(m, L, k).start()
 
     def b4(m, L):
@@ -894,7 +896,7 @@
         return cp(("dd", L), s["SND"], s["TOT"], at(dc=1))
 
     def backward(L, xin, dF, mid):
-        gain_a, gain_f = gains(L)
+        gain_a, gain_f = s["GN"][L, 0:1, :], s["GN"][L, 1:2, :]
         dlow = dF.astype(BF)
         if L == 1:
             s["IGB"][...] = dlow
@@ -971,7 +973,7 @@
         def _():
             dkv_up(L).wait_recv()
             s["DKV"][...] = (s["DKV"][...].astype(F32) + s["DS"][...].astype(F32)).astype(BF)
-            for k in (1, 2, 3):
+            for k in (2, 1, 3):
                 dkv_x(L, k).start()
 
         mid[2]()

time: 178 us -> 175 us (0.983)
  Pallas kernels: 176 us -> 174 us
    pallas_call x1, Pallas kernels: 174 us -> 172 us  [body(): pl.pallas_call(mega, out_shape=shapes, in_specs=[any_, any_, pl.BlockSpec...]
where the time goes in v4:
time: 175 us
  Pallas kernels  174 us (99%)
    pallas_call x1, Pallas kernels, body(): pl.pallas_call(mega, out_shape=shapes, in_specs=[any_, any_, pl.BlockSpec...  172 us

profile of v4, /device:TPU:1, one launch (start us, length us, event | category | flops | bytes accessed | tf_op | source)
XLA Modules:
  0.0 175.2 jit_solution(9508145086466196268)
XLA Ops:
  0.6 171.6 %layers.1 = (bf16[1,2,576,128]{3,2,1,0:T(8,128)(2,1)}, bf16[1,2,576,128]{3,2,1,0:T(8,128)(2,1)}, f32[1,72]{1,0:T(1,128)}, f32[1,72,576]{2,1,0:T(8,128)}, f32[1,7...) custom-call(bf16[2,576,128]{2,1,0:T(8,128)(2,1)} %bitcast.4, ...), custom_call_target="tpu_custom_call" | custom-call | tf_op jit(solution)/shard_map/layers/pallas_call | solution.py:1185
  172.2 2.7 %results.1 = (bf16[1,2,576,128]{3,2,1,0:T(8,128)(2,1)}, bf16[1,2,576,128]{3,2,1,0:T(8,128)(2,1)}, f32[1,72]{1,0:T(1,128)}, f32[1,72,576]{2,1,0:T(8,128)}, f32[1,...) custom-call(bf16[1,2,576,128]{3,2,1,0:T(8,128)(2,1)} %get-tuple-elem, ...), custom_call_target="tpu_custom_call" | custom-call | tf_op jit(solution)/shard_map/results/pallas_call | solution.py:1198
